TPU v7x, 256 devices: a whole 4x4x8 slice. The times are simulated.
256 devices in a mesh: rep: 2 (over x_hi), ew: 8 (over z), ns: 16 (over x_lo, y, core).
Axes of the slice: x: 4 (x_hi: 2, x_lo: 2; x = x_hi * 2 + x_lo), y: 4, z: 8, core: 2. Of those that a mesh axis runs over, the one named last changes fastest.
Arguments:
- fields: bfloat16 [2, 192, 32, 2048], P('rep', None, 'ew', 'ns'), may hold values from -6 to 6
- cotangent: bfloat16 [2, 192, 32, 2048], P('rep', None, 'ew', 'ns'), may hold values from -6 to 6
- land_mask: int32 [32, 2048], P('ew', 'ns'), may hold values 0 or 1
- stretch_index: int32 [1], replicated, may hold values from 0 to 23
- depth_kernel: float32 [2, 2, 192, 49], P('rep'), may hold values from -0.875 to 0.875
- norm_gain: float32 [2, 2, 192], P('rep'), may hold values from 0.5 to 1.5
- norm_bias: float32 [2, 2, 192], P('rep'), may hold values from -3 to 3
- weight_in: float32 [2, 2, 192, 768], P('rep'), may hold values from -0.4375 to 0.4375
- bias_in: float32 [2, 2, 768], P('rep'), may hold values from -3 to 3
- weight_out: float32 [2, 2, 768, 192], P('rep'), may hold values from -0.21875 to 0.21875
- bias_out: float32 [2, 2, 192], P('rep'), may hold values from -3 to 3
- layer_scale: float32 [2, 2, 192], P('rep'), may hold values from 0.5 to 1.5
- anchor_in: float32 [2, 192, 768], replicated, may hold values from -0.4375 to 0.4375
- anchor_out: float32 [2, 768, 192], replicated, may hold values from -0.21875 to 0.21875
Outputs:
- new_kernel: float32 [2, 2, 192, 49], P('rep')
- new_weight_in: float32 [2, 2, 192, 768], P('rep')
- new_weight_out: float32 [2, 2, 768, 192], P('rep')
- cycle_in: float32 [2, 192, 64], P('rep')
- cycle_out: float32 [2, 64, 192], P('rep')
All inputs are finite; a program needn't handle non-finite values. No bound on the sum of `land_mask` on one device may be relied on, other than what follows from the above.
Results may differ from a plain program's by a relative error of at most 0.007.
Values may be sent and summed in bfloat16 or wider, within the bound.
A program may use at most 128 MiB of HBM per device.

v0:
```python
import math

import jax
import jax.numpy as jnp
from jax import lax
from jax.sharding import PartitionSpec as P

HID = 768
STRETCHES = 12


EPSILON = 1e-06
STEP_RATE = 0.1
GELU_C = 0.7978845608028654


def extended(cells, sides, width, closed):
    for axis, dim in sides:
        count = lax.axis_size(axis)
        ends = count if closed else count - 1
        head = lax.slice_in_dim(cells, 0, width, axis=dim)
        tail = lax.slice_in_dim(cells, cells.shape[dim] - width, cells.shape[dim], axis=dim)
        cells = jnp.concatenate(
            [
                lax.ppermute(tail, axis, [(i, (i + 1) % count) for i in range(ends)]),
                cells,
                lax.ppermute(head, axis, [((i + 1) % count, i) for i in range(ends)]),
            ],
            axis=dim,
        )
    return cells


def passed_along(block, axis, distance):
    devices = range(lax.axis_size(axis))
    route = [((i - distance) % len(devices), i) for i in devices]
    return lax.ppermute(block, axis, route)


def depthwise(padded, kernel, extent_x, extent_y):
    summed = jnp.zeros((padded.shape[0], extent_x, extent_y), jnp.float32)
    for tap_row in range(7):
        for tap_col in range(7):
            weight_tap = kernel[:, tap_row * 7 + tap_col][:, None, None]
            summed = (
                summed
                + weight_tap * padded[:, tap_row : tap_row + extent_x, tap_col : tap_col + extent_y]
            )
    return summed


def kernel_grad(padded, conv_grad):
    extent_x = conv_grad.shape[1]
    extent_y = conv_grad.shape[2]
    columns = []
    for tap_row in range(7):
        for tap_col in range(7):
            window = padded[:, tap_row : tap_row + extent_x, tap_col : tap_col + extent_y]
            columns.append(jnp.sum(conv_grad * window, axis=(1, 2)))
    return jnp.stack(columns, axis=1)


def gelu_pair(hidden_pre):
    tanh_arg = GELU_C * (hidden_pre + 0.044715 * hidden_pre * hidden_pre * hidden_pre)
    tanh_val = jnp.tanh(tanh_arg)
    gelu_value = 0.5 * hidden_pre * (1.0 + tanh_val)
    gelu_slope = 0.5 * (1.0 + tanh_val) + 0.5 * hidden_pre * (
        1.0 - tanh_val * tanh_val
    ) * GELU_C * (1.0 + 3.0 * 0.044715 * hidden_pre * hidden_pre)
    return (gelu_value, gelu_slope)


def pointwise_forward(
    conv_out,
    residual,
    ocean_cells,
    gain_vec,
    shift_bias,
    weight_in_b,
    bias_vec_in,
    weight_out_b,
    bias_vec_out,
    scale_vec,
):
    centered = conv_out - jnp.mean(conv_out, axis=0, keepdims=True)
    inv_std = lax.rsqrt(jnp.mean(centered * centered, axis=0, keepdims=True) + EPSILON)
    normed = centered * inv_std
    normed_b = (normed * gain_vec[:, None] + shift_bias[:, None]).astype(jnp.bfloat16)
    hidden_pre = (
        jnp.dot(weight_in_b.T, normed_b, preferred_element_type=jnp.float32) + bias_vec_in[:, None]
    )
    active, gelu_slope = gelu_pair(hidden_pre)
    active_b = active.astype(jnp.bfloat16)
    branch = (
        jnp.dot(weight_out_b.T, active_b, preferred_element_type=jnp.float32)
        + bias_vec_out[:, None]
    )
    output = ocean_cells[None, :] * (residual + scale_vec[:, None] * branch)
    return (output, (normed, inv_std, normed_b, gelu_slope, active_b))


def pointwise_backward(
    flow_grad, kept_values, ocean_cells, gain_vec, weight_in_b, weight_out_b, scale_vec
):
    normed, inv_std, normed_b, gelu_slope, active_b = kept_values
    masked = ocean_cells[None, :] * flow_grad
    branch_grad = (masked * scale_vec[:, None]).astype(jnp.bfloat16)
    grad_out_w = jnp.dot(active_b, branch_grad.T, preferred_element_type=jnp.float32)
    active_grad = jnp.dot(weight_out_b, branch_grad, preferred_element_type=jnp.float32)
    hidden_grad = (active_grad * gelu_slope).astype(jnp.bfloat16)
    grad_in_w = jnp.dot(normed_b, hidden_grad.T, preferred_element_type=jnp.float32)
    normed_grad = (
        jnp.dot(weight_in_b, hidden_grad, preferred_element_type=jnp.float32) * gain_vec[:, None]
    )
    mean_grad = jnp.mean(normed_grad, axis=0, keepdims=True)
    mean_cross = jnp.mean(normed_grad * normed, axis=0, keepdims=True)
    conv_grad = inv_std * (normed_grad - mean_grad - normed * mean_cross)
    return (conv_grad, masked, grad_in_w, grad_out_w)


def extend_forward(field):
    partial_rim = extended(field, (("ns", 2),), 3, False)
    return extended(partial_rim, (("ew", 1),), 3, True)


def extend_backward(field):
    partial_rim = extended(field.astype(jnp.bfloat16), (("ns", 2),), 3, False).astype(field.dtype)
    return extended(partial_rim.astype(jnp.bfloat16), (("ew", 1),), 3, True).astype(
        partial_rim.dtype
    )


def reduce_update(grad_kernel, grad_in_w, grad_out_w, kernel, weight_inner, weight_outer):
    summed_kernel, summed_in, summed_out = lax.psum(
        (grad_kernel, grad_in_w, grad_out_w), ("ew", "ns")
    )
    return (
        kernel - STEP_RATE * summed_kernel,
        weight_inner - STEP_RATE * summed_in,
        weight_outer - STEP_RATE * summed_out,
    )


def body(
    fields,
    cotangent,
    land_mask,
    stretch_index,
    depth_kernel,
    norm_gain,
    norm_bias,
    weight_in,
    bias_in,
    weight_out,
    bias_out,
    layer_scale,
    anchor_in,
    anchor_out,
):
    channels = fields.shape[1]
    extent_x = fields.shape[2]
    extent_y = fields.shape[3]
    cell_count = extent_x * extent_y
    layers_count = depth_kernel.shape[1]
    rescale = 1.0 / math.sqrt(extent_x * lax.axis_size("ew") * extent_y * lax.axis_size("ns"))
    ocean_cells = land_mask.astype(jnp.float32).reshape(cell_count)
    current = fields[0]
    stored = []
    for layer_index in range(layers_count):
        padded = extend_forward(current).astype(jnp.float32)
        conv_out = depthwise(padded, depth_kernel[0, layer_index], extent_x, extent_y)
        layer_in = current.astype(jnp.float32).reshape(channels, cell_count)
        output, kept_values = pointwise_forward(
            conv_out.reshape(channels, cell_count),
            layer_in,
            ocean_cells,
            norm_gain[0, layer_index],
            norm_bias[0, layer_index],
            weight_in[0, layer_index].astype(jnp.bfloat16),
            bias_in[0, layer_index],
            weight_out[0, layer_index].astype(jnp.bfloat16),
            bias_out[0, layer_index],
            layer_scale[0, layer_index],
        )
        stored.append((padded, kept_values))
        current = output.reshape(channels, extent_x, extent_y).astype(jnp.bfloat16)
    flowing = cotangent[0].astype(jnp.float32).reshape(channels, cell_count) * rescale
    new_kernels = [None] * layers_count
    new_inner = [None] * layers_count
    new_outer = [None] * layers_count
    for layer_index in reversed(range(layers_count)):
        padded, kept_values = stored[layer_index]
        kernel = depth_kernel[0, layer_index]
        conv_grad, masked, grad_in_w, grad_out_w = pointwise_backward(
            flowing,
            kept_values,
            ocean_cells,
            norm_gain[0, layer_index],
            weight_in[0, layer_index].astype(jnp.bfloat16),
            weight_out[0, layer_index].astype(jnp.bfloat16),
            layer_scale[0, layer_index],
        )
        conv_field = conv_grad.reshape(channels, extent_x, extent_y)
        grad_kernel = kernel_grad(padded, conv_field)
        if layer_index > 0:
            spread = extend_backward(conv_field)
            flowing = masked + depthwise(spread, kernel[:, ::-1], extent_x, extent_y).reshape(
                channels, cell_count
            )
        updated = reduce_update(
            grad_kernel,
            grad_in_w,
            grad_out_w,
            kernel,
            weight_in[0, layer_index],
            weight_out[0, layer_index],
        )
        new_kernels[layer_index] = updated[0]
        new_inner[layer_index] = updated[1]
        new_outer[layer_index] = updated[2]
    inner_stack = jnp.stack(new_inner)
    outer_stack = jnp.stack(new_outer)
    choose = stretch_index[0]
    span_width = HID // STRETCHES
    layer_pick = choose // STRETCHES
    start = choose % STRETCHES * span_width
    diff_inner = lax.dynamic_index_in_dim(
        anchor_in, layer_pick, 0, False
    ) - lax.dynamic_index_in_dim(inner_stack, layer_pick, 0, False)
    diff_outer = lax.dynamic_index_in_dim(
        anchor_out, layer_pick, 0, False
    ) - lax.dynamic_index_in_dim(outer_stack, layer_pick, 0, False)
    stretch_inner = lax.dynamic_slice_in_dim(diff_inner, start, span_width, 1)
    stretch_outer = lax.dynamic_slice_in_dim(diff_outer, start, span_width, 0)
    cycle_inner, cycle_outer = passed_along((stretch_inner, stretch_outer), "rep", 1)
    return (
        jnp.stack(new_kernels)[None],
        inner_stack[None],
        outer_stack[None],
        cycle_inner[None],
        cycle_outer[None],
    )


def solution(mesh):
    in_specs = (
        P("rep", None, "ew", "ns"),
        P("rep", None, "ew", "ns"),
        P("ew", "ns"),
        P(),
        P("rep", None, None, None),
        P("rep", None, None),
        P("rep", None, None),
        P("rep", None, None, None),
        P("rep", None, None),
        P("rep", None, None, None),
        P("rep", None, None),
        P("rep", None, None),
        P(),
        P(),
    )
    out_specs = (
        P("rep", None, None, None),
        P("rep", None, None, None),
        P("rep", None, None, None),
        P("rep", None, None),
        P("rep", None, None),
    )
    return jax.shard_map(body, mesh=mesh, in_specs=in_specs, out_specs=out_specs, check_vma=False)
```

profile of v0, /device:TPU:1, one launch (start us, length us, event | category | flops | bytes accessed | tf_op | source)
XLA Modules:
  0.0 2137.0 jit_solution(7404874652153961897)
XLA Ops:
  8.3 4.7 collective-permute-start
  13.1 1.9 collective-permute-start.1
  24.6 4.0 collective-permute-start.3
  29.9 2.3 collective-permute-done.2
  32.3 3.8 fusion.122
  39.9 5.6 collective-permute-start.4
  45.5 1.9 collective-permute-start.5
  50.6 3.0 collective-permute-start.7
  55.5 1.8 collective-permute-done.6
  57.9 4.6 fusion.121
  70.2 1.8 fusion.82
  77.7 4.4 collective-permute-start.8
  82.3 2.1 collective-permute-start.9
  86.0 4.3 stack.427
  90.5 2.3 collective-permute-start.10
  94.3 1.9 fusion.93
  99.1 5.2 fusion.77
  112.0 1.7 multiply_reduce_fusion.49
  115.4 3.2 fusion.94
  118.9 6.4 stack.376
  127.3 933.1 %all-reduce.5.cloned.1.call-done = (f32[192,49]{0,1:T(8,128)}, f32[192,49]{0,1:T(8,128)}) async-done(((f32[192,49]{0,1:T(8,128)}, f32[192,49]{0,1:T(8,128)}), (f32[192,49]{0,1:T(8,128)}, f32[192,49]{0,1:T(8,128)})) %all-reduce.5.cloned.1.call-update) | async-done | bytes 75280 | tf_op jit(solution)/shard_map/psum | solution.py:134
  1062.9 1052.8 %all-reduce.7.cloned.1.call-done = (f32[192,768]{1,0:T(8,128)}, f32[192,768]{1,0:T(8,128)}, f32[768,192]{0,1:T(8,128)}, f32[768,192]{0,1:T(8,128)}) async-done(((f32[192,768]{1,0:T(8,128)}, f32[192,768]{1,0:T(8,128)}, f32[768,192]{0,1:T(8,128)}, f32[768,192]{0,1:T(8,128)}), (f32[192,768]{1,0:T(8,128)}, f32[192,768]{1,0:T(8,128)}, f32[768,192]{0,1:T(8,128)}, ...) | async-done | bytes 2359312 | tf_op jit(solution)/shard_map/psum | solution.py:134
  2119.3 2.5 collective-permute-start.12
  2125.9 3.0 collective-permute-done.13
  (446 shorter events, 61.3 us)
Async XLA Ops:
  7.2 15.0 copy-start.168
  7.2 1053.2 %all-reduce.5.cloned.1.call-start = ((), (), s32[]{:S(2)}) async-start(), calls=%async_computation | async-start | bytes 229376 | tf_op jit(solution)/shard_map/psum | solution.py:134
  8.3 20.4 copy-start.169
  8.3 20.9 copy-start.22
  8.3 14.4 collective-permute-start
  13.1 9.7 collective-permute-start.1
  17.0 20.9 copy-start.167
  18.7 38.7 %copy-start.34 = (f32[192,1]{0,1:T(1,128)}, f32[192,1]{0,1:T(1,128)S(1)}, u32[]{:S(2)}) copy-start(f32[192,1]{0,1:T(1,128)S(1)} %get-tuple-element.154) | copy-start | bytes 2308
  20.2 17.6 copy-start.127
  21.3 26.7 %copy-start.6 = (bf16[1,192,4,128]{1,3,2,0:T(8,128)(2,1)}, bf16[1,192,4,128]{1,3,2,0:T(8,128)(2,1)S(1)}, u32[]{:S(2)}) copy-start(bf16[1,192,4,128]{1,3,2,0:T(8,128)(2,1)S(1)} %copy.29) | copy-start | bytes 589828
  22.9 9.3 collective-permute-start.2
  24.6 7.6 collective-permute-start.3
  39.9 9.0 collective-permute-start.4
  45.5 5.0 collective-permute-start.5
  50.5 6.7 collective-permute-start.6
  50.6 6.7 collective-permute-start.7
  77.7 12.6 collective-permute-start.8
  82.3 8.1 collective-permute-start.9
  90.5 6.4 collective-permute-start.10
  93.1 5.4 collective-permute-start.11
  125.3 1990.4 %all-reduce.7.cloned.1.call-start = ((), (), s32[]{:S(2)}) async-start(), calls=%async_computation.1 | async-start | bytes 4718592 | tf_op jit(solution)/shard_map/psum | solution.py:134
  126.6 933.8 %copy-start.25 = (f32[1,1,192,49]{2,1,3,0:T(1,128)S(1)}, f32[1,1,192,49]{2,1,3,0:T(1,128)}, u32[]{:S(2)}) copy-start(f32[1,1,192,49]{2,1,3,0:T(1,128)} %copy-done.24) | copy-start | bytes 112900
  2119.3 6.6 collective-permute-start.12
  2124.2 4.7 collective-permute-start.13
  (164 other events, 682.6 us)
Sparse Core Ops, SparseCore 0:
  125.5 934.8 all-reduce.4
  1064.1 1051.5 all-reduce.6
where the time goes:
time: 2140 us
  waiting for transfers between devices  2000 us (93%)
  other arithmetic  41 us (2%)
  starting transfers between devices  36.2 us (2%)
  local copies, waits for them, and re-layouts  31.5 us (1%)
    psum x2, waiting for transfers between devices, reduce_update(): lax.psum((grad_kernel, grad_in_w, grad_out_w), ('ew', 'ns'))  1990 us
  transfers between devices with their start and end apart: 16, of which 8 were waited for; matrix products, arithmetic and copies ran while one was open for 1% of the time, Pallas kernels for 0%

commit v1 on v0

v1 whole, which is shorter than its diff:
```python
import functools

import jax
import jax.numpy as jnp
from jax import lax
from jax.experimental import pallas as pl
from jax.experimental.pallas import tpu as pltpu
from jax.sharding import PartitionSpec as P

EPSILON = 1e-06
STEP_RATE = 0.1
GELU_C = 0.7978845608028654
GELU_D = 0.044715

MESH = pl.DeviceIdType.MESH
F32 = jnp.float32
BF16 = jnp.bfloat16
C = 192
HID = 768
LAYERS = 2
CX = 4
CY = 128
CELLS = CX * CY
ROWS = CX + 6
BLOCKS = C // 8
FOLD = 4
FOLDED = C // FOLD
XY = 8
EW = 8
NS = 16
ZT = 2
GAIN, SHIFT, OUT_BIAS, SCALE = 49, 50, 51, 52
SHARES = (10, 9)


def remote(src, dst, send_sem, recv_sem, device):
    return pltpu.make_async_remote_copy(
        src_ref=src,
        dst_ref=dst,
        send_sem=send_sem,
        recv_sem=recv_sem,
        device_id=device,
        device_id_type=MESH,
    )


def lanes_of(shape):
    return lax.broadcasted_iota(jnp.int32, shape, 1)


def dot(left, right):
    return jnp.dot(left, right, preferred_element_type=F32)


def dot_cells(left, right):
    return lax.dot_general(left, right, (((1,), (1,)), ((), ())), preferred_element_type=F32)


def rounded(cells):
    return cells.astype(BF16).astype(F32)


class Place:
    def __init__(self):
        self.rep = lax.axis_index("rep")
        self.z = lax.axis_index("ew")
        self.ns = lax.axis_index("ns")
        self.core = lax.rem(self.ns, 2)
        self.chip = self.ns // 2

    def twin(self):
        return (self.rep, self.z, 2 * self.chip + 1 - self.core)

    def in_plane(self, step):
        return (self.rep, self.z, 2 * lax.rem(self.chip + step, XY) + self.core)

    def on_line(self, step):
        return (self.rep, lax.rem(self.z + step, EW), self.ns)

    def beside(self, step_z, step_ns):
        return (
            self.rep,
            lax.rem(self.z + EW + step_z, EW),
            lax.rem(self.ns + NS + step_ns, NS),
        )


AROUND = [(dz, dn) for dn in (1, -1) for dz in (-1, 0, 1)]


class Halo:
    def __init__(self, place, turn, out_rows, out_edges, in_rows, in_edges, sent, came):
        self.place = place
        self.out_rows = out_rows.at[turn]
        self.out_edges = out_edges.at[turn]
        self.in_rows = in_rows.at[turn]
        self.in_edges = in_edges.at[turn]
        self.sent = sent.at[turn]
        self.came = came.at[turn]
        self.copies = []

    def start(self, source):
        lane = lanes_of((FOLDED, CY))
        group = lane // 32
        inside = lane % 32
        folded = jnp.zeros((FOLDED, CY), F32)
        for x in range(CX):
            row = source(x)
            self.out_rows[x] = row.astype(BF16)
            for part in range(FOLD):
                piece = row[FOLDED * part : FOLDED * (part + 1), :]
                base = 32 * part + 8 * x
                low = pltpu.roll(piece, base, 1) if base else piece
                high = pltpu.roll(piece, (base + 8) % CY, 1) if (base + 8) % CY else piece
                here = group == part
                folded = jnp.where(here & (inside >= 8 * x) & (inside < 8 * x + 3), low, folded)
                folded = jnp.where(here & (inside >= 8 * x + 5) & (inside < 8 * x + 8), high, folded)
        self.out_edges[...] = folded.astype(BF16)
        place = self.place
        rows = [
            remote(
                self.out_rows.at[pl.ds(1, 3)],
                self.in_rows.at[0],
                self.sent.at[0],
                self.came.at[0],
                place.beside(1, 0),
            ),
            remote(
                self.out_rows.at[pl.ds(0, 3)],
                self.in_rows.at[1],
                self.sent.at[1],
                self.came.at[1],
                place.beside(-1, 0),
            ),
        ]
        edges = []
        for number, (dz, dn) in enumerate(AROUND):
            side = 0 if dn == 1 else 1
            edges.append(
                remote(
                    self.out_edges,
                    self.in_edges.at[side, 1 - dz],
                    self.sent.at[2 + number],
                    self.came.at[2 + number],
                    place.beside(dz, dn),
                )
            )
        self.copies = edges + rows
        for copy in self.copies:
            copy.start()

    def finish(self, main, halo):
        for copy in self.copies:
            copy.wait_recv()
        for row in range(3):
            main[row] = self.in_rows[0, row].astype(F32)
            main[CX + 3 + row] = self.in_rows[1, row].astype(F32)
        keep_left = (self.place.ns > 0).astype(F32)
        keep_right = (self.place.ns < NS - 1).astype(F32)
        lane = lanes_of((FOLDED, CY))
        for index in range(3):
            left = self.in_edges[0, index].astype(F32) * keep_left
            right = self.in_edges[1, index].astype(F32) * keep_right
            for x in range(CX):
                row = (x - 1, x + 3, x + 7)[index]
                if (index == 0 and x == 0) or (index == 2 and x == 3):
                    continue
                for part in range(FOLD):
                    base = 32 * part + 8 * x
                    from_left = pltpu.roll(left, (120 - base) % CY, 1) if base != 120 else left
                    from_right = pltpu.roll(right, (CY - base) % CY, 1) if base else right
                    halo[row, FOLDED * part : FOLDED * (part + 1), :] = jnp.where(
                        lane < 64, from_right, from_left
                    )

    def close(self):
        for copy in self.copies:
            copy.wait_send()


def shifted(main, halo, distance, lane):
    if distance == 0:
        return main
    if distance > 0:
        chosen = jnp.where(lane < distance, halo, main)
    else:
        chosen = jnp.where(lane >= CY + distance, halo, main)
    return pltpu.roll(chosen, (-distance) % CY, 1)


def depthwise(main, halo, taps, out, keep, reverse):
    @pl.loop(0, BLOCKS)
    def _(block):
        at = pl.ds(block * 8, 8)
        lane = lanes_of((8, CY))
        weights = taps[at, :]
        total = [jnp.zeros((8, CY), F32) for _ in range(CX)]
        for col in range(7):
            rows = []
            for row in range(ROWS):
                moved = shifted(main[row, at, :], halo[row, at, :], col - 3, lane)
                if keep is not None and col != 3:
                    keep[col, row, at, :] = moved
                rows.append(moved)
            for tap_row in range(7):
                tap = 7 * tap_row + col
                if reverse:
                    tap = 48 - tap
                weight = jnp.broadcast_to(weights[:, tap : tap + 1], (8, CY))
                for x in range(CX):
                    total[x] = total[x] + weight * rows[x + tap_row]
        for x in range(CX):
            out[x, at, :] = total[x]


def kernel_grad(windows, conv_grad, out, lane_base, first):
    @pl.loop(0, BLOCKS)
    def _(block):
        at = pl.ds(block * 8, 8)
        lane = lanes_of((8, CY))
        grads = [conv_grad[x, at, :] for x in range(CX)]
        result = jnp.zeros((8, CY), F32)
        for col in range(7):
            rows = [windows[col, row, at, :] for row in range(ROWS)]
            for tap_row in range(7):
                total = grads[0] * rows[tap_row]
                for x in range(1, CX):
                    total = total + grads[x] * rows[x + tap_row]
                tap = 7 * tap_row + col
                result = jnp.where(
                    lane == tap + lane_base, jnp.sum(total, axis=1, keepdims=True), result
                )
        if first:
            out[at, :] = result
        else:
            out[at, :] = out[at, :] + result


class Sum:
    def __init__(self, place, tiles, send1, recv1, own, send2, recv2, send3, recv3, total, sems):
        self.place = place
        self.tiles = tiles
        self.send1, self.recv1, self.own = send1, recv1, own
        self.send2, self.recv2, self.send3, self.recv3 = send2, recv2, send3, recv3
        self.total = total
        self.sems = sems
        self.started = []

    def go(self, copy):
        copy.start()
        self.started.append(copy)
        return copy

    def pair(self, phase, step):
        return self.sems[2 * phase].at[step], self.sems[2 * phase + 1].at[step]

    def pack(self, grads, extra, half, dst):
        @pl.loop(0, 12)
        def _(row):
            for col in range(6):
                dst[row * 6 + col] = grads[
                    half, pl.ds(row * 16, 16), 128 * col : 128 * (col + 1)
                ].astype(dst.dtype)

        if extra is not None:
            for block in range(6):
                dst[72 + block] = extra[pl.ds(half * 96 + 16 * block, 16), :].astype(dst.dtype)
            dst[pl.ds(78, 2)] = jnp.zeros((2, 16, 128), dst.dtype)

    def share(self, step):
        return pl.ds(self.tiles * lax.rem(self.place.chip + step, XY), self.tiles)

    def start(self, grads, extra):
        core = self.place.core
        self.pack(grads, extra, 1 - core, self.send1)
        self.first = []
        for step in list(range(1, XY)) + [0]:
            part = self.share(step)
            copy = remote(
                self.send1.at[part], self.recv1.at[part], *self.pair(0, step), self.place.twin()
            )
            self.first.append((step, self.go(copy)))
        self.pack(grads, extra, core, self.own)

    def to_plane(self):
        self.second = []
        for step, copy in self.first:
            copy.wait_recv()
            part = self.own[self.share(step)] + self.recv1[self.share(step)].astype(F32)
            if step == 0:
                self.own[pl.ds(0, self.tiles)] = part
            else:
                self.send2[step - 1] = part.astype(BF16)
                copy = remote(
                    self.send2.at[step - 1],
                    self.recv2.at[step - 1],
                    *self.pair(1, step - 1),
                    self.place.in_plane(step),
                )
                self.second.append(self.go(copy))

    def stretch(self, step):
        return pl.ds(ZT * lax.rem(self.place.z + step, EW), ZT)

    def to_line(self):
        own = pl.ds(0, self.tiles)
        for copy in self.second:
            copy.wait_recv()
        part = self.own[own]
        for step in range(XY - 1):
            part = part + self.recv2[step].astype(F32)
        self.own[own] = part
        rest = pl.ds(self.tiles, EW * ZT - self.tiles)
        self.own[rest] = jnp.zeros((EW * ZT - self.tiles, 16, 128), F32)
        self.send3[pl.ds(0, EW * ZT)] = self.own[pl.ds(0, EW * ZT)].astype(BF16)
        self.third = []
        for step in range(1, EW):
            copy = remote(
                self.send3.at[self.stretch(step)],
                self.recv3.at[step - 1],
                *self.pair(2, step - 1),
                self.place.on_line(step),
            )
            self.third.append(self.go(copy))

    def back_line(self):
        for copy in self.third:
            copy.wait_recv()
        part = self.own[self.stretch(0)]
        for step in range(EW - 1):
            part = part + self.recv3[step].astype(F32)
        here = self.total.at[self.place.core, self.place.chip, self.stretch(0)]
        here[...] = part.astype(BF16)
        self.fourth = []
        for step in range(1, EW):
            copy = remote(here, here, *self.pair(3, step - 1), self.place.on_line(step))
            self.fourth.append(self.go(copy))

    def back_plane(self):
        for copy in self.fourth:
            copy.wait_recv()
        mine = self.total.at[self.place.core, self.place.chip]
        self.fifth = []
        for step in range(1, XY):
            copy = remote(mine, mine, *self.pair(4, step - 1), self.place.in_plane(step))
            self.fifth.append(self.go(copy))
        self.sixth = [self.go(remote(mine, mine, *self.pair(5, 0), self.place.twin()))]

    def back_twin(self):
        for step, copy in enumerate(self.fifth):
            copy.wait_recv()
            came = self.total.at[
                self.place.core, lax.rem(self.place.chip + XY - (step + 1), XY)
            ]
            copy = remote(came, came, *self.pair(5, step + 1), self.place.twin())
            self.sixth.append(self.go(copy))
        for copy in self.sixth:
            copy.wait_recv()

    def close(self):
        for copy in self.started:
            copy.wait_send()


def step_kernel(
    x_in,
    cot_in,
    mask_in,
    rows_in,
    bias_in,
    win,
    wout_t,
    total0,
    total1,
    cols,
    bias_col,
    win_b,
    win_tb,
    wout_tb,
    wout_b,
    windows,
    halo,
    conv,
    normed,
    inv_std,
    norm_b,
    hidden,
    slope,
    act_b,
    flow,
    back_b,
    hid_b,
    conv_grad,
    grad_w,
    grad_k,
    out_rows,
    out_edges,
    in_rows,
    in_edges,
    send1,
    recv1,
    own,
    send2,
    recv2,
    send3,
    recv3,
    halo_sent,
    halo_came,
    *sems,
):
    place = Place()
    barrier = pltpu.get_barrier_semaphore()
    peers = [place.twin()]
    peers += [place.in_plane(d) for d in range(1, XY)]
    peers += [place.on_line(d) for d in range(1, EW)]
    peers += [place.beside(dz, dn) for dz, dn in AROUND]
    for peer in peers:
        pl.semaphore_signal(barrier, inc=1, device_id=peer, device_id_type=MESH)

    def lanes(x):
        return slice(CY * x, CY * (x + 1))

    for layer in range(LAYERS):
        cols[layer] = rows_in[layer].T[:C]
        win_b[layer] = win[layer].astype(BF16)
        win_tb[layer] = win[layer].T.astype(BF16)
        wout_tb[layer] = wout_t[layer].astype(BF16)
        wout_b[layer] = wout_t[layer].T.astype(BF16)
    bias_col[...] = bias_in[...].T
    pl.semaphore_wait(barrier, len(peers))

    halos = [
        Halo(place, turn, out_rows, out_edges, in_rows, in_edges, halo_sent, halo_came)
        for turn in range(3)
    ]
    sums = [
        Sum(
            place,
            SHARES[layer],
            send1.at[layer],
            recv1.at[layer],
            own.at[layer],
            send2.at[layer, :, pl.ds(0, SHARES[layer])],
            recv2.at[layer, :, pl.ds(0, SHARES[layer])],
            send3.at[layer],
            recv3.at[layer],
            (total0, total1)[layer],
            sems[12 * layer : 12 * (layer + 1)],
        )
        for layer in range(LAYERS)
    ]

    ocean = [mask_in[x : x + 1, :].astype(F32) for x in range(CX)]

    def column(layer, which):
        return cols[layer, :, which : which + 1]

    def forward(layer):
        main = windows.at[layer, 3]
        halos[layer].finish(main, halo)
        depthwise(main, halo, cols.at[layer], conv, windows.at[layer], False)
        for x in range(CX):
            cells = conv[x]
            centered = cells - jnp.mean(cells, axis=0, keepdims=True)
            inv = lax.rsqrt(jnp.mean(centered * centered, axis=0, keepdims=True) + EPSILON)
            unit = centered * inv
            inv_std[layer, x : x + 1, :] = inv
            normed[layer, x] = unit
            norm_b[layer, :, lanes(x)] = (
                unit * column(layer, GAIN) + column(layer, SHIFT)
            ).astype(BF16)
        hidden[...] = dot(win_tb[layer], norm_b[layer])

        @pl.loop(0, HID // 16)
        def _(block):
            at = pl.ds(block * 16, 16)
            pre = hidden[at, :] + bias_col[at, layer : layer + 1]
            square = pre * pre
            bend = GELU_C * GELU_D * square
            gate = 0.5 + 0.5 * jnp.tanh(pre * (GELU_C + bend))
            value = pre * gate
            act_b[layer, at, :] = value.astype(BF16)
            slope[layer, at, :] = gate + 2.0 * value * (1.0 - gate) * (GELU_C + 3.0 * bend)

    def output(layer):
        branch = dot(wout_tb[layer], act_b[layer])
        for x in range(CX):
            inner = branch[:, lanes(x)] + column(layer, OUT_BIAS)
            value = ocean[x] * (windows[layer, 3, 3 + x] + column(layer, SCALE) * inner)
            windows[layer + 1, 3, 3 + x] = rounded(value)

    def backward(layer):
        for x in range(CX):
            masked = ocean[x] * flow[x]
            flow[x] = masked
            back_b[:, lanes(x)] = (masked * column(layer, SCALE)).astype(BF16)
        grad_w[layer, 1] = dot_cells(back_b[...], act_b[layer])
        hidden[...] = dot(wout_b[layer], back_b[...])

        @pl.loop(0, HID // 16)
        def _(block):
            at = pl.ds(block * 16, 16)
            hid_b[at, :] = (hidden[at, :] * slope[layer, at, :]).astype(BF16)

        grad_w[layer, 0] = dot_cells(norm_b[layer], hid_b[...])
        norm_grad = dot(win_b[layer], hid_b[...])
        for x in range(CX):
            part = norm_grad[:, lanes(x)] * column(layer, GAIN)
            unit = normed[layer, x]
            mean_grad = jnp.mean(part, axis=0, keepdims=True)
            mean_cross = jnp.mean(part * unit, axis=0, keepdims=True)
            conv_grad[x] = inv_std[layer, x : x + 1, :] * (part - mean_grad - unit * mean_cross)

    for x in range(CX):
        windows[0, 3, 3 + x] = x_in[x].astype(F32)
    halos[0].start(lambda x: windows[0, 3, 3 + x])
    forward(0)
    output(0)
    halos[1].start(lambda x: windows[1, 3, 3 + x])
    for x in range(CX):
        flow[x] = cot_in[x].astype(F32) * (1.0 / 256.0)
    forward(1)
    backward(1)
    halos[2].start(lambda x: conv_grad[x])
    sums[1].start(grad_w.at[1], None)
    kernel_grad(windows.at[1], conv_grad, grad_k, 64, True)
    sums[1].to_plane()
    main = windows.at[1, 3]
    for x in range(CX):
        main[3 + x] = conv_grad[x]
    halos[2].finish(main, halo)
    depthwise(main, halo, cols.at[1], conv, None, True)
    for x in range(CX):
        flow[x] = flow[x] + conv[x]
    sums[1].to_line()
    backward(0)
    sums[1].back_line()
    kernel_grad(windows.at[0], conv_grad, grad_k, 0, False)
    sums[0].start(grad_w.at[0], grad_k)
    sums[1].back_plane()
    sums[0].to_plane()
    sums[1].back_twin()
    sums[0].to_line()
    sums[0].back_line()
    sums[0].back_plane()
    sums[0].back_twin()
    for each in halos + sums:
        each.close()


def whole_step(x, cot, mask, rows, bias, win, wout_t):
    dma = pltpu.SemaphoreType.DMA
    vmem = pltpu.VMEM
    tiles = XY * max(SHARES)
    total = jax.ShapeDtypeStruct((2, XY, EW * ZT, 16, 128), BF16)
    sums = ([dma((8,))] * 2 + [dma((7,))] * 8 + [dma((8,))] * 2) * LAYERS
    return pl.pallas_call(
        step_kernel,
        out_shape=[total, total],
        in_specs=[pl.BlockSpec(memory_space=pltpu.VMEM)] * 7,
        out_specs=[pl.BlockSpec(memory_space=pltpu.VMEM)] * 2,
        scratch_shapes=[
            vmem((LAYERS, C, 128), F32),
            vmem((HID, 128), F32),
            vmem((LAYERS, C, HID), BF16),
            vmem((LAYERS, HID, C), BF16),
            vmem((LAYERS, C, HID), BF16),
            vmem((LAYERS, HID, C), BF16),
            vmem((LAYERS, 7, ROWS, C, CY), F32),
            vmem((ROWS, C, CY), F32),
            vmem((CX, C, CY), F32),
            vmem((LAYERS, CX, C, CY), F32),
            vmem((LAYERS, CX, CY), F32),
            vmem((LAYERS, C, CELLS), BF16),
            vmem((HID, CELLS), F32),
            vmem((LAYERS, HID, CELLS), F32),
            vmem((LAYERS, HID, CELLS), BF16),
            vmem((CX, C, CY), F32),
            vmem((C, CELLS), BF16),
            vmem((HID, CELLS), BF16),
            vmem((CX, C, CY), F32),
            vmem((LAYERS, 2, C, HID), F32),
            vmem((C, 128), F32),
            vmem((3, CX, C, CY), BF16),
            vmem((3, FOLDED, CY), BF16),
            vmem((3, 2, 3, C, CY), BF16),
            vmem((3, 2, 3, FOLDED, CY), BF16),
            vmem((LAYERS, tiles, 16, 128), BF16),
            vmem((LAYERS, tiles, 16, 128), BF16),
            vmem((LAYERS, tiles, 16, 128), F32),
            vmem((LAYERS, XY - 1, max(SHARES), 16, 128), BF16),
            vmem((LAYERS, XY - 1, max(SHARES), 16, 128), BF16),
            vmem((LAYERS, EW * ZT, 16, 128), BF16),
            vmem((LAYERS, EW - 1, ZT, 16, 128), BF16),
            dma((3, 8)),
            dma((3, 8)),
        ]
        + sums,
        compiler_params=pltpu.CompilerParams(
            collective_id=0, has_side_effects=True, vmem_limit_bytes=56 * 2**20
        ),
    )(x, cot, mask, rows, bias, win, wout_t)


def update_kernel(
    index, total0, total1, win, wout_t, anchor_in, anchor_out, kernel, new_in, new_out, new_k, cycle
):
    for layer, total in enumerate((total0, total1)):
        tiles = SHARES[layer]
        for tile in range(72):
            row, col = tile // 6, tile % 6
            at = (layer, slice(16 * row, 16 * (row + 1)), slice(128 * col, 128 * (col + 1)))
            spot = (tile // tiles, tile % tiles)
            new_in[at] = win[at] - STEP_RATE * total[(0,) + spot].astype(F32)
            new_out[at] = wout_t[at] - STEP_RATE * total[(1,) + spot].astype(F32)
    tiles = SHARES[0]
    grads = []
    for half in range(2):
        for block in range(6):
            tile = 72 + block
            grads.append(total0[half, tile // tiles, tile % tiles].astype(F32))
    taps = jnp.concatenate(grads, axis=0).T
    for layer in range(LAYERS):
        new_k[layer] = kernel[layer] - STEP_RATE * taps[64 * layer : 64 * layer + 49, :]
    layer = index[0] // 12
    within = lax.rem(index[0], 12)
    block = pl.ds(pl.multiple_of(within // 2 * 128, 128), 128)
    odd = lax.rem(within, 2) == 1
    first = anchor_in[layer, :, block] - new_in[layer, :, block]
    second = anchor_out[layer, :, block] - new_out[layer, :, block]
    turned = pltpu.roll(first, 64, 1)
    first = jnp.where(odd, turned, first)
    turned = pltpu.roll(second, 64, 1)
    second = jnp.where(odd, second, turned)
    lane = lanes_of((C, 128))
    cycle[...] = jnp.where(lane < 64, first, second).T


def update(index, total0, total1, win, wout_t, anchor_in, anchor_out, kernel):
    weights = jax.ShapeDtypeStruct((LAYERS, C, HID), F32)
    return pl.pallas_call(
        update_kernel,
        out_shape=[
            weights,
            weights,
            jax.ShapeDtypeStruct((LAYERS, 49, C), F32),
            jax.ShapeDtypeStruct((128, C), F32),
        ],
        in_specs=[pl.BlockSpec(memory_space=pltpu.SMEM)]
        + [pl.BlockSpec(memory_space=pltpu.VMEM)] * 7,
        out_specs=[pl.BlockSpec(memory_space=pltpu.VMEM)] * 4,
        compiler_params=pltpu.CompilerParams(vmem_limit_bytes=40 * 2**20),
    )(index, total0, total1, win, wout_t, anchor_in, anchor_out, kernel)


def body(
    fields,
    cotangent,
    land_mask,
    stretch_index,
    depth_kernel,
    norm_gain,
    norm_bias,
    weight_in,
    bias_in,
    weight_out,
    bias_out,
    layer_scale,
    anchor_in,
    anchor_out,
):
    x = fields[0].transpose(1, 0, 2)
    cot = cotangent[0].transpose(1, 0, 2)
    taps = depth_kernel[0].transpose(0, 2, 1)
    vectors = jnp.stack([norm_gain[0], norm_bias[0], bias_out[0], layer_scale[0]], axis=1)
    rows = jnp.concatenate([taps, vectors], axis=1)
    rows = jnp.pad(rows, ((0, 0), (0, 128 - rows.shape[1]), (0, 256 - C)))
    bias = jnp.pad(bias_in[0], ((0, 128 - LAYERS), (0, 0)))
    win = weight_in[0]
    wout_t = weight_out[0].transpose(0, 2, 1)
    total0, total1 = whole_step(x, cot, land_mask, rows, bias, win, wout_t)
    new_in, new_out, new_k, cycle = update(
        stretch_index,
        total0,
        total1,
        win,
        wout_t,
        anchor_in,
        anchor_out.transpose(0, 2, 1),
        taps,
    )
    cycle = lax.ppermute(cycle, "rep", [(0, 1), (1, 0)])
    return (
        new_k.transpose(0, 2, 1)[None],
        new_in[None],
        new_out.transpose(0, 2, 1)[None],
        cycle[:64].T[None],
        cycle[64:][None],
    )


def solution(mesh):
    in_specs = (
        P("rep", None, "ew", "ns"),
        P("rep", None, "ew", "ns"),
        P("ew", "ns"),
        P(),
        P("rep", None, None, None),
        P("rep", None, None),
        P("rep", None, None),
        P("rep", None, None, None),
        P("rep", None, None),
        P("rep", None, None, None),
        P("rep", None, None),
        P("rep", None, None),
        P(),
        P(),
    )
    out_specs = (
        P("rep", None, None, None),
        P("rep", None, None, None),
        P("rep", None, None, None),
        P("rep", None, None),
        P("rep", None, None),
    )
    return jax.shard_map(body, mesh=mesh, in_specs=in_specs, out_specs=out_specs, check_vma=False)
```

time: 2140 us -> 119 us (0.06)
  waiting for transfers between devices: 2000 us -> 3.45 us
  Pallas kernels: 0 us -> 101 us
  other arithmetic: 41 us -> 0 us
  starting transfers between devices: 36.2 us -> 2.45 us
    psum x2 -> x0, waiting for transfers between devices: 1990 us -> none  [reduce_update(): lax.psum((grad_kernel, grad_in_w, grad_out_w), ('ew', 'ns'))]
    pallas_call x0 -> x2, Pallas kernels: none -> 101 us  [the longest x1 99.5 us: whole_step(): pl.pallas_call(step_kernel, out_shape=[total, total], in_specs=[pl.BlockS...]
    ppermute x14 -> x1, starting transfers between devices: 36.1 us -> 2.45 us  [body(): cycle = lax.ppermute(cycle, 'rep', [(0, 1), (1, 0)])]
  transfers between devices with their start and end apart: 16 -> 1, of which waited for: 8 -> 1; matrix products, arithmetic and copies ran while one was open for 1% -> 1% of each run, Pallas kernels for 0% -> 0%
where the time goes in v1:
time: 119 us
  Pallas kernels  101 us (85%)
  local copies, waits for them, and re-layouts  10.5 us (9%)
  waiting for transfers between devices  3.45 us (3%)
  starting transfers between devices  2.45 us (2%)
  between operations  1.41 us (1%)
    pallas_call x1, Pallas kernels, whole_step(): pl.pallas_call(step_kernel, out_shape=[total, total], in_specs=[pl.BlockS...  99.5 us
    unnamed x18, local copies, waits for them, and re-layouts  4.06 us
    ppermute x1, waiting for transfers between devices, body(): cycle = lax.ppermute(cycle, 'rep', [(0, 1), (1, 0)])  3.45 us
    another operation x4, local copies, waits for them, and re-layouts, body(): jnp.stack([norm_gain[0], norm_bias[0], bias_out[0], layer_scale[0]], axis=1)  2.73 us
    ppermute x1, starting transfers between devices, body(): cycle = lax.ppermute(cycle, 'rep', [(0, 1), (1, 0)])  2.45 us
  transfers between devices with their start and end apart: 1, of which 1 were waited for; matrix products, arithmetic and copies ran while one was open for 1% of the time, Pallas kernels for 0%

profile of v1, /device:TPU:1, one launch (start us, length us, event | category | flops | bytes accessed | tf_op | source)
XLA Modules:
  0.0 118.9 jit_solution(13227056919171206607)
XLA Ops:
  0.6 0.0 copy-start.6
  0.6 0.0 copy-start.7
  1.3 0.7 stack_squeeze.12
  2.0 0.7 stack_squeeze.13
  2.7 0.7 stack_squeeze.14
  3.4 0.7 stack_squeeze.15
  4.1 0.9 copy.26
  5.0 0.7 pad.8.rows_in
  5.8 1.5 %pad.9.bias_in = f32[128,768]{1,0:T(8,128)} pad(f32[2,768]{1,0:T(2,128)} %bitcast.40, f32[]{:T(128)} %constant.2.clone.1), padding=0_126x0_0 | pad | bytes 399364 | tf_op jit(solution)/shard_map/jit(_pad)/pad | solution.py:678
  7.2 0.0 copy-done.6
  7.2 0.8 copy_bitcast_fusion
  8.0 99.5 %shard_map.173 = (bf16[2,8,16,16,128]{4,3,2,1,0:T(8,128)(2,1)}, bf16[2,8,16,16,128]{4,3,2,1,0:T(8,128)(2,1)}) custom-call(bf16[4,192,128]{2,1,0:T(8,128)(2,1)} %get-tuple-element.25.x_in, bf16[4,192,128]{2,1,0:T(8,128)(2,1)} %get-tuple-element.24.cot_in, s32[4,128]{1,0:T(4,128)} %mask_in.1, f32[2,128,256]{2,1,0:T(8,128)} %pad.8.rows_in, ...), custom_call_target="tpu_custom_call" | custom-call | tf_op jit(solution)/shard_map/pallas_call | solution.py:557
  107.5 0.0 copy-done.3
  107.5 0.0 copy-done.2
  107.5 0.0 copy-done
  107.5 0.0 copy-done.1
  107.6 0.0 copy-start.4
  107.6 1.2 %copy-done.4 = bf16[2,8,16,16,128]{4,3,2,1,0:T(8,128)(2,1)S(1)} copy-done((bf16[2,8,16,16,128]{4,3,2,1,0:T(8,128)(2,1)S(1)}, bf16[2,8,16,16,128]{4,3,2,1,0:T(8,128)(2,1)}, u32[]{:S(2)}) %copy-start.4) | copy-done | bytes 1048600
  108.8 1.2 %copy-done.5 = bf16[2,8,16,16,128]{4,3,2,1,0:T(8,128)(2,1)S(1)} copy-done((bf16[2,8,16,16,128]{4,3,2,1,0:T(8,128)(2,1)S(1)}, bf16[2,8,16,16,128]{4,3,2,1,0:T(8,128)(2,1)}, u32[]{:S(2)}) %copy-start.5) | copy-done | bytes 1048600
  110.0 1.7 %shard_map.174 = (f32[2,192,768]{2,1,0:T(8,128)}, f32[2,192,768]{2,1,0:T(8,128)}, f32[2,49,192]{2,1,0:T(8,128)S(1)}, f32[128,192]{1,0:T(8,128)S(1)}) custom-call(s32[1]{0:T(128)S(6)} %copy.27.index, bf16[2,8,16,16,128]{4,3,2,1,0:T(8,128)(2,1)S(1)} %copy-done.4, bf16[2,8,16,16,128]{4,3,2,1,0:T(8,128)(2,1)S(1)} %copy-done.5, f32[2,192,768]{2,1,0:T(8,128)S(1)} %bitcast.33, ...), custom_call_target="tpu_custom_call" | custom-call | tf_op jit(solution)/shard_map/pallas_call | solution.py:641
  111.7 2.5 %collective-permute-start = (f32[128,192]{1,0:T(8,128)S(1)}, f32[128,192]{1,0:T(8,128)S(1)}, u32[]{:S(2)}, u32[]{:S(2)}) collective-permute-start(f32[128,192]{1,0:T(8,128)S(1)} %get-tuple-element.16), channel_id=1, source_target_pairs={{0,128},{128,0},{1,129},{129,1},{2,130},{130,2},{3,131},{131,3},{4... | collective-permute-start | bytes 294920 | tf_op jit(solution)/shard_map/ppermute | solution.py:692
  114.1 0.7 copy.22
  114.8 3.5 %collective-permute-done = f32[128,192]{1,0:T(8,128)S(1)} collective-permute-done((f32[128,192]{1,0:T(8,128)S(1)}, f32[128,192]{1,0:T(8,128)S(1)}, u32[]{:S(2)}, u32[]{:S(2)}) %collective-permute-start) | collective-permute-done | bytes 98336 | tf_op jit(solution)/shard_map/ppermute | solution.py:692
  118.3 0.7 slice_bitcast_fusion
  (7 shorter events, 0.0 us)
Async XLA Ops:
  0.6 6.6 %copy-start.6 = (bf16[1,192,4,128]{3,2,1,0:T(4,128)(2,1)S(1)}, bf16[1,192,4,128]{3,2,1,0:T(4,128)(2,1)}, u32[]{:S(2)}) copy-start(bf16[1,192,4,128]{3,2,1,0:T(4,128)(2,1)} %param.15) | copy-start | bytes 589828
  0.6 6.6 %copy-start.7 = (bf16[1,192,4,128]{3,2,1,0:T(4,128)(2,1)S(1)}, bf16[1,192,4,128]{3,2,1,0:T(4,128)(2,1)}, u32[]{:S(2)}) copy-start(bf16[1,192,4,128]{3,2,1,0:T(4,128)(2,1)} %param.14) | copy-start | bytes 589828
  5.0 102.5 %copy-start.3 = (f32[2,768,192]{1,2,0:T(8,128)S(1)}, f32[2,768,192]{1,2,0:T(8,128)}, u32[]{:S(2)}) copy-start(f32[2,768,192]{1,2,0:T(8,128)} %param.27) | copy-start | bytes 3538948
  7.2 100.3 %copy-start.2 = (f32[2,192,768]{2,1,0:T(8,128)S(1)}, f32[2,192,768]{2,1,0:T(8,128)}, u32[]{:S(2)}) copy-start(f32[2,192,768]{2,1,0:T(8,128)} %anchor_in.1) | copy-start | bytes 3538948
  8.0 99.5 %copy-start = (f32[1,2,192,768]{3,2,1,0:T(8,128)S(1)}, f32[1,2,192,768]{3,2,1,0:T(8,128)}, u32[]{:S(2)}) copy-start(f32[1,2,192,768]{3,2,1,0:T(8,128)} %param.21) | copy-start | bytes 3538948
  8.0 99.5 %copy-start.1 = (f32[1,2,768,192]{2,3,1,0:T(8,128)S(1)}, f32[1,2,768,192]{2,3,1,0:T(8,128)}, u32[]{:S(2)}) copy-start(f32[1,2,768,192]{2,3,1,0:T(8,128)} %param.23) | copy-start | bytes 3538948
  107.6 1.2 %copy-start.4 = (bf16[2,8,16,16,128]{4,3,2,1,0:T(8,128)(2,1)S(1)}, bf16[2,8,16,16,128]{4,3,2,1,0:T(8,128)(2,1)}, u32[]{:S(2)}) copy-start(bf16[2,8,16,16,128]{4,3,2,1,0:T(8,128)(2,1)} %get-tuple-element.11.total0) | copy-start | bytes 3145732
  108.8 1.2 %copy-start.5 = (bf16[2,8,16,16,128]{4,3,2,1,0:T(8,128)(2,1)S(1)}, bf16[2,8,16,16,128]{4,3,2,1,0:T(8,128)(2,1)}, u32[]{:S(2)}) copy-start(bf16[2,8,16,16,128]{4,3,2,1,0:T(8,128)(2,1)} %get-tuple-element.12.total1) | copy-start | bytes 3145732
  111.7 6.6 %collective-permute-start = (f32[128,192]{1,0:T(8,128)S(1)}, f32[128,192]{1,0:T(8,128)S(1)}, u32[]{:S(2)}, u32[]{:S(2)}) collective-permute-start(f32[128,192]{1,0:T(8,128)S(1)} %get-tuple-element.16), channel_id=1, source_target_pairs={{0,128},{128,0},{1,129},{129,1},{2,130},{130,2},{3,131},{131,3},{4... | collective-permute-start | bytes 294920 | tf_op jit(solution)/shard_map/ppermute | solution.py:692

commit v2 on v1

v2 whole, which is shorter than its diff:
```python
import jax
import jax.numpy as jnp
from jax import lax
from jax.experimental import pallas as pl
from jax.experimental.pallas import tpu as pltpu
from jax.sharding import PartitionSpec as P

EPSILON = 1e-06
STEP_RATE = 0.1
GELU_C = 0.7978845608028654
GELU_D = 0.044715

MESH = pl.DeviceIdType.MESH
F32 = jnp.float32
BF16 = jnp.bfloat16
C = 192
HID = 768
LAYERS = 2
CX = 4
CY = 128
CELLS = CX * CY
ROWS = CX + 6
BLOCKS = C // 8
FOLD = 4
FOLDED = C // FOLD
XY = 8
EW = 8
SHIFTED = (0, 1, 2, 4, 5, 6)
NS = 16
ZT = 2
GAIN, SHIFT, OUT_BIAS, SCALE = 49, 50, 51, 52
SHARE = 9
MAIN = 3 * ROWS + 3
SHARES = (10, 9)


def remote(src, dst, send_sem, recv_sem, device):
    return pltpu.make_async_remote_copy(
        src_ref=src,
        dst_ref=dst,
        send_sem=send_sem,
        recv_sem=recv_sem,
        device_id=device,
        device_id_type=MESH,
    )


def lanes_of(shape):
    return lax.broadcasted_iota(jnp.int32, shape, 1)


def dot(left, right):
    return jnp.dot(left, right, preferred_element_type=F32)


def dot_cells(left, right):
    return lax.dot_general(left, right, (((1,), (1,)), ((), ())), preferred_element_type=F32)


class Place:
    def __init__(self):
        self.rep = lax.axis_index("rep")
        self.z = lax.axis_index("ew")
        self.ns = lax.axis_index("ns")
        self.core = lax.rem(self.ns, 2)
        self.chip = self.ns // 2

    def twin(self):
        return (self.rep, self.z, 2 * self.chip + 1 - self.core)

    def in_plane(self, step):
        return (self.rep, self.z, 2 * lax.rem(self.chip + step, XY) + self.core)

    def on_line(self, step):
        return (self.rep, lax.rem(self.z + step, EW), self.ns)

    def beside(self, step_z, step_ns):
        return (
            self.rep,
            lax.rem(self.z + EW + step_z, EW),
            lax.rem(self.ns + NS + step_ns, NS),
        )


AROUND = [(dz, dn) for dn in (1, -1) for dz in (-1, 0, 1)]


class Halo:
    def __init__(self, place, turn, rows, out_edges, in_rows, in_edges, sent, came):
        self.place = place
        self.rows = rows
        self.out_edges = out_edges.at[turn]
        self.in_rows = in_rows.at[turn]
        self.in_edges = in_edges.at[turn]
        self.sent = sent.at[turn]
        self.came = came.at[turn]
        self.row_copies = []
        self.edge_copies = []

    def start(self):
        place = self.place
        for number, (first, step) in enumerate(((1, 1), (0, -1))):
            copy = remote(
                self.rows.at[pl.ds(first, 3)],
                self.in_rows.at[number],
                self.sent.at[number],
                self.came.at[number],
                place.beside(step, 0),
            )
            copy.start()
            self.row_copies.append(copy)
        slot = ((lanes_of((FOLDED, CY)) + 4) % CY) // 8
        folded = jnp.zeros((FOLDED, CY), F32)
        for x in range(CX):
            row = self.rows[x].astype(F32)
            for part in range(FOLD):
                piece = row[FOLDED * part : FOLDED * (part + 1), :]
                number = 4 * part + x
                moved = pltpu.roll(piece, 8 * number, 1) if number else piece
                folded = jnp.where(slot == number, moved, folded)
        self.out_edges[...] = folded.astype(BF16)
        for number, (dz, dn) in enumerate(AROUND):
            side = 0 if dn == 1 else 1
            copy = remote(
                self.out_edges,
                self.in_edges.at[side, 1 - dz],
                self.sent.at[2 + number],
                self.came.at[2 + number],
                place.beside(dz, dn),
            )
            copy.start()
            self.edge_copies.append(copy)

    def near(self, shifts, halo, windows):
        for copy in self.edge_copies:
            copy.wait_recv()
        keep_left = (self.place.ns > 0).astype(F32)
        keep_right = (self.place.ns < NS - 1).astype(F32)
        low = (lanes_of((FOLDED, CY)) + 4) % 8 < 4
        for index in range(3):
            edges = jnp.where(
                low,
                self.in_edges[0, index].astype(F32) * keep_left,
                self.in_edges[1, index].astype(F32) * keep_right,
            )
            for x in range(CX):
                row = (x - 1, x + 3, x + 7)[index]
                if (index == 0 and x == 0) or (index == 2 and x == 3):
                    continue
                for part in range(FOLD):
                    number = 4 * part + x
                    moved = pltpu.roll(edges, CY - 8 * number, 1) if number else edges
                    halo[row, FOLDED * part : FOLDED * (part + 1), :] = moved.astype(BF16)

        self.shift(self.rows, 3, CX, shifts, halo, windows)

    def shift(self, rows, first, count, shifts, halo, windows):
        cells = jnp.concatenate(
            [
                rows[...].reshape(count * C, CY),
                halo[first : first + count].reshape(count * C, CY),
            ],
            axis=1,
        )
        moved = dot(cells, shifts[...])
        for place, col in enumerate(SHIFTED):
            start = col * ROWS + first
            windows[start : start + count] = moved[:, CY * place : CY * (place + 1)].reshape(
                count, C, CY
            )

    def far(self, shifts, halo, windows):
        for copy in self.row_copies:
            copy.wait_recv()
        for side, first in ((0, 0), (1, CX + 3)):
            self.shift(self.in_rows.at[side], first, 3, shifts, halo, windows)
            start = 3 * ROWS + first
            windows[start : start + 3] = self.in_rows[side].astype(F32)

    def close(self):
        for copy in self.row_copies + self.edge_copies:
            copy.wait_send()


def shift_matrix():
    source = lax.broadcasted_iota(jnp.int32, (2 * CY, CY), 0)
    lane = lanes_of((2 * CY, CY))
    parts = []
    for col in SHIFTED:
        wanted = lane + (col - 3)
        hit = (source == wanted) | (source == wanted + 2 * CY)
        parts.append(hit.astype(F32).astype(BF16))
    return jnp.concatenate(parts, axis=1)


def spread_taps(taps, out):
    @pl.loop(0, BLOCKS, unroll=4)
    def _(block):
        at = pl.ds(block * 8, 8)
        weights = taps[at, :]
        for tap in range(49):
            out[tap, at, :] = jnp.broadcast_to(weights[:, tap : tap + 1], (8, CY))


def depthwise(windows, spread, out, reverse, own):
    @pl.loop(0, BLOCKS, unroll=2)
    def _(block):
        at = pl.ds(block * 8, 8)
        total = [None if own else out[x, at, :] for x in range(CX)]
        used = [row for row in range(ROWS) if (3 <= row < 3 + CX) == own]
        for col in range(7):
            rows = {row: windows[col * ROWS + row, at, :] for row in used}
            part = [None] * CX
            for tap_row in range(7):
                if not any(x + tap_row in rows for x in range(CX)):
                    continue
                tap = 7 * tap_row + col
                weight = spread[48 - tap if reverse else tap, at, :]
                for x in range(CX):
                    if x + tap_row in rows:
                        term = weight * rows[x + tap_row]
                        part[x] = term if part[x] is None else part[x] + term
            for x in range(CX):
                if part[x] is not None:
                    total[x] = part[x] if total[x] is None else total[x] + part[x]
        for x in range(CX):
            out[x, at, :] = total[x]


def kernel_grad(windows, conv_grad, out, lane_base, first):
    @pl.loop(0, BLOCKS, unroll=4)
    def _(block):
        at = pl.ds(block * 8, 8)
        lane = lanes_of((8, CY))
        grads = [conv_grad[x, at, :] for x in range(CX)]
        result = jnp.zeros((8, CY), F32)
        for col in range(7):
            rows = [windows[col * ROWS + row, at, :] for row in range(ROWS)]
            for tap_row in range(7):
                total = grads[0] * rows[tap_row]
                for x in range(1, CX):
                    total = total + grads[x] * rows[x + tap_row]
                tap = 7 * tap_row + col
                result = jnp.where(
                    lane == tap + lane_base, jnp.sum(total, axis=1, keepdims=True), result
                )
        if first:
            out[at, :] = result
        else:
            out[at, :] = out[at, :] + result


class Sum:
    def __init__(
        self, place, tiles, send1, recv1, own, mine, send2, recv2, send3, recv3, line, total, sems
    ):
        self.place = place
        self.tiles = tiles
        self.send1, self.recv1, self.own, self.mine = send1, recv1, own, mine
        self.send2, self.recv2, self.send3, self.recv3 = send2, recv2, send3, recv3
        self.line = line
        self.total = total
        self.sems = sems
        self.started = []
        self.extra = None

    def go(self, copy):
        copy.start()
        self.started.append(copy)
        return copy

    def pair(self, phase, step):
        return self.sems[2 * phase].at[step], self.sems[2 * phase + 1].at[step]

    def pack(self, grads, half, dst):
        @pl.loop(0, 12, unroll=2)
        def _(row):
            for col in range(6):
                dst[row * 6 + col] = grads[
                    half, pl.ds(row * 16, 16), 128 * col : 128 * (col + 1)
                ].astype(dst.dtype)

    def pack_extra(self, extra, half, dst):
        for block in range(6):
            dst[72 + block] = extra[pl.ds(half * 96 + 16 * block, 16), :].astype(dst.dtype)
        dst[78:80] = jnp.zeros((2, 16, 128), dst.dtype)

    def chunk(self, step):
        return lax.rem(self.place.chip + step, XY)

    def share(self, step):
        return pl.ds(SHARE * self.chunk(step), SHARE)

    def start(self, grads):
        core = self.place.core
        self.pack(grads, 1 - core, self.send1)
        self.first = []
        for step in list(range(1, XY)) + [0]:
            part = self.share(step)
            copy = remote(
                self.send1.at[part], self.recv1.at[part], *self.pair(0, step), self.place.twin()
            )
            self.first.append((step, self.go(copy)))
        self.pack(grads, core, self.own)

    def start_extra(self, extra):
        core = self.place.core
        self.pack_extra(extra, 1 - core, self.send1)
        part = pl.ds(72, 8)
        self.extra = self.go(
            remote(self.send1.at[part], self.recv1.at[part], *self.pair(0, 8), self.place.twin())
        )
        self.pack_extra(extra, core, self.own)

    def to_plane(self):
        self.second = []
        if self.extra is not None:
            self.extra.wait_recv()
        self.mine[...] = jnp.zeros_like(self.mine)
        for step, copy in self.first:
            copy.wait_recv()
            part = self.own[self.share(step)] + self.recv1[self.share(step)].astype(F32)
            if self.extra is not None:
                spot = 72 + self.chunk(step)
                more = self.own[spot] + self.recv1[spot].astype(F32)
            if step == 0:
                self.mine[0:SHARE] = part
                if self.extra is not None:
                    self.mine[SHARE] = more
            else:
                self.send2[step - 1, 0:SHARE] = part.astype(BF16)
                if self.extra is not None:
                    self.send2[step - 1, SHARE] = more.astype(BF16)
                copy = remote(
                    self.send2.at[step - 1, pl.ds(0, self.tiles)],
                    self.recv2.at[step - 1, pl.ds(0, self.tiles)],
                    *self.pair(1, step - 1),
                    self.place.in_plane(step),
                )
                self.second.append(self.go(copy))

    def stretch(self, step):
        return pl.ds(ZT * lax.rem(self.place.z + step, EW), ZT)

    def to_line(self):
        for copy in self.second:
            copy.wait_recv()
        part = self.mine[0 : self.tiles]
        for step in range(XY - 1):
            part = part + self.recv2[step, 0 : self.tiles].astype(F32)
        self.mine[0 : self.tiles] = part
        self.send3[...] = self.mine[...].astype(BF16)
        self.third = []
        for step in range(1, EW):
            copy = remote(
                self.send3.at[self.stretch(step)],
                self.recv3.at[step - 1],
                *self.pair(2, step - 1),
                self.place.on_line(step),
            )
            self.third.append(self.go(copy))

    def back_line(self):
        for copy in self.third:
            copy.wait_recv()
        part = self.mine[self.stretch(0)]
        for step in range(EW - 1):
            part = part + self.recv3[step].astype(F32)
        here = self.line.at[self.stretch(0)]
        here[...] = part.astype(BF16)
        self.fourth = []
        for step in range(1, EW):
            copy = remote(here, here, *self.pair(3, step - 1), self.place.on_line(step))
            self.fourth.append(self.go(copy))

    def back_plane(self):
        for copy in self.fourth:
            copy.wait_recv()
        core, chip = self.place.core, self.place.chip
        used = pl.ds(0, self.tiles)
        share, mine = self.line.at[used], self.total.at[core, chip, used]
        self.fifth = []
        for step in range(1, XY):
            copy = remote(share, mine, *self.pair(4, step - 1), self.place.in_plane(step))
            self.fifth.append(self.go(copy))
        self.sixth = [self.go(remote(share, mine, *self.pair(5, 0), self.place.twin()))]
        mine[...] = share[...]

    def back_twin(self):
        for step, copy in enumerate(self.fifth):
            copy.wait_recv()
            came = self.total.at[
                self.place.core,
                lax.rem(self.place.chip + XY - (step + 1), XY),
                pl.ds(0, self.tiles),
            ]
            copy = remote(came, came, *self.pair(5, step + 1), self.place.twin())
            self.sixth.append(self.go(copy))
        for copy in self.sixth:
            copy.wait_recv()

    def close(self):
        for copy in self.started:
            copy.wait_send()


def step_kernel(
    index,
    x_in,
    cot_in,
    mask_in,
    taps_in,
    gain_in,
    shift_in,
    out_bias_in,
    scale_in,
    bias_in,
    win_hbm,
    wout_hbm,
    anchor_in,
    anchor_out,
    totals,
    cycle_came,
    cells_t,
    x_rows,
    cot_rows,
    weights,
    anchors,
    ahead,
    rows_t,
    cols,
    bias_col,
    win_b,
    win_tb,
    wout_tb,
    wout_b,
    shifts,
    spread,
    windows,
    halo,
    conv,
    normed,
    inv_std,
    norm_b,
    hidden,
    slope,
    act_b,
    flow,
    back_b,
    hid_b,
    conv_grad,
    grad_w,
    grad_k,
    out_rows,
    out_edges,
    in_rows,
    in_edges,
    send1,
    recv1,
    own,
    mine,
    send2,
    recv2,
    send3,
    recv3,
    line,
    cycle_out,
    halo_sent,
    halo_came,
    weight_sem,
    anchor_sem,
    cycle_sem,
    *sems,
):
    place = Place()
    barrier = pltpu.get_barrier_semaphore()
    partner = (1 - place.rep, place.z, place.ns)
    peers = [place.twin(), partner]
    peers += [place.in_plane(d) for d in range(1, XY)]
    peers += [place.on_line(d) for d in range(1, EW)]
    peers += [place.beside(dz, dn) for dz, dn in AROUND]
    for peer in peers:
        pl.semaphore_signal(barrier, inc=1, device_id=peer, device_id_type=MESH)
    fetched = [
        pltpu.make_async_copy(anchor_in, anchors.at[0], anchor_sem.at[0]),
        pltpu.make_async_copy(anchor_out, anchors.at[1], anchor_sem.at[1]),
    ]
    loaded = [
        pltpu.make_async_copy(win_hbm, weights.at[0], weight_sem.at[0]),
        pltpu.make_async_copy(wout_hbm, weights.at[1], weight_sem.at[1]),
    ]
    for copy in loaded + fetched:
        copy.start()
    win, wout_t = weights.at[0], weights.at[1]

    def lanes(x):
        return slice(CY * x, CY * (x + 1))

    halos = [
        Halo(
            place,
            turn,
            (x_rows, out_rows.at[0], out_rows.at[1])[turn],
            out_edges,
            in_rows,
            in_edges,
            halo_sent,
            halo_came,
        )
        for turn in range(3)
    ]
    sums = [
        Sum(
            place,
            SHARES[layer],
            send1.at[layer],
            recv1.at[layer],
            own.at[layer],
            mine.at[layer],
            send2.at[layer],
            recv2.at[layer],
            send3.at[layer],
            recv3.at[layer],
            line.at[layer],
            totals.at[layer],
            sems[12 * layer : 12 * (layer + 1)],
        )
        for layer in range(LAYERS)
    ]

    def prepare(layer):
        rows_t[...] = jnp.zeros_like(rows_t)
        rows_t[0:49, 0:C] = taps_in[:, layer, :]
        for row, vector in (
            (GAIN, gain_in),
            (SHIFT, shift_in),
            (OUT_BIAS, out_bias_in),
            (SCALE, scale_in),
        ):
            rows_t[row : row + 1, 0:C] = vector[layer : layer + 1, :]
        cols[layer] = rows_t[...].T[:C]
        win_tb[layer] = win[layer].T.astype(BF16)
        wout_tb[layer] = wout_t[layer].astype(BF16)
        spread_taps(cols.at[layer], spread.at[layer])

    def prepare_back(layer):
        win_b[layer] = win[layer].astype(BF16)
        wout_b[layer] = wout_t[layer].T.astype(BF16)

    ocean = [mask_in[x : x + 1, :].astype(F32) for x in range(CX)]

    def column(layer, which):
        return cols[layer, :, which : which + 1]

    def forward(layer):
        halos[layer].near(shifts, halo, windows.at[layer])
        depthwise(windows.at[layer], spread.at[layer], conv, False, True)
        halos[layer].far(shifts, halo, windows.at[layer])
        depthwise(windows.at[layer], spread.at[layer], conv, False, False)
        for x in range(CX):
            cells = conv[x]
            centered = cells - jnp.mean(cells, axis=0, keepdims=True)
            inv = lax.rsqrt(jnp.mean(centered * centered, axis=0, keepdims=True) + EPSILON)
            unit = centered * inv
            inv_std[layer, x : x + 1, :] = inv
            normed[layer, x] = unit
            norm_b[layer, :, lanes(x)] = (
                unit * column(layer, GAIN) + column(layer, SHIFT)
            ).astype(BF16)
        hidden[...] = dot(win_tb[layer], norm_b[layer])

        @pl.loop(0, HID // 192)
        def _(block):
            at = pl.ds(block * 192, 192)
            pre = hidden[at, :] + bias_col[at, layer : layer + 1]
            bend = (GELU_C * GELU_D) * (pre * pre)
            gate = 0.5 + 0.5 * jnp.tanh(pre * (GELU_C + bend))
            value = pre * gate
            act_b[layer, at, :] = value.astype(BF16)
            slope[layer, at, :] = gate + 2.0 * value * (1.0 - gate) * (GELU_C + 3.0 * bend)

    def output(layer):
        branch = dot(wout_tb[layer], act_b[layer])
        for x in range(CX):
            inner = branch[:, lanes(x)] + column(layer, OUT_BIAS)
            value = ocean[x] * (windows[layer, MAIN + x] + column(layer, SCALE) * inner)
            value = value.astype(BF16)
            out_rows[0, x] = value
            windows[layer + 1, MAIN + x] = value.astype(F32)

    def backward(layer):
        for x in range(CX):
            masked = ocean[x] * flow[x]
            flow[x] = masked
            back_b[:, lanes(x)] = (masked * column(layer, SCALE)).astype(BF16)
        grad_w[layer, 1] = dot_cells(back_b[...], act_b[layer])
        hidden[...] = dot(wout_b[layer], back_b[...])

        @pl.loop(0, HID // 192)
        def _(block):
            at = pl.ds(block * 192, 192)
            hid_b[at, :] = (hidden[at, :] * slope[layer, at, :]).astype(BF16)

        grad_w[layer, 0] = dot_cells(norm_b[layer], hid_b[...])

    def backward_norm(layer):
        norm_grad = dot(win_b[layer], hid_b[...])
        for x in range(CX):
            part = norm_grad[:, lanes(x)] * column(layer, GAIN)
            unit = normed[layer, x]
            mean_grad = jnp.mean(part, axis=0, keepdims=True)
            mean_cross = jnp.mean(part * unit, axis=0, keepdims=True)
            value = inv_std[layer, x : x + 1, :] * (part - mean_grad - unit * mean_cross)
            conv_grad[x] = value
            if layer > 0:
                out_rows[1, x] = value.astype(BF16)

    def by_rows(cells_in, out):
        cells_t[...] = cells_in[...].astype(F32)
        for x in range(CX):
            out[x] = cells_t[pl.ds(x, C, stride=CX), :].astype(BF16)

    def block_at(shape):
        return jnp.full(shape, index[0] // 2, jnp.int32)

    def joined(first, second):
        odd = jnp.full((C, 128), lax.rem(index[0], 2), jnp.int32) == 1
        first = jnp.where(odd, pltpu.roll(first, 64, 1), first)
        second = jnp.where(odd, second, pltpu.roll(second, 64, 1))
        return jnp.where(lanes_of((C, 128)) < 64, first, second)

    def stretch_ahead():
        for copy in fetched:
            copy.wait()
        chosen = [jnp.zeros((C, 128), F32), jnp.zeros((C, 128), F32)]
        for which in range(LAYERS):
            for col in range(6):
                hit = block_at((C, 128)) == 6 * which + col
                for mat, weights in enumerate((win, wout_t)):
                    at = (which, slice(0, C), slice(128 * col, 128 * (col + 1)))
                    chosen[mat] = jnp.where(hit, anchors[(mat,) + at] - weights[at], chosen[mat])
        ahead[...] = joined(*chosen)

    by_rows(x_in, x_rows)
    pl.semaphore_wait(barrier, len(peers))
    halos[0].start()
    for x in range(CX):
        windows[0, MAIN + x] = x_rows[x].astype(F32)
    shifts[...] = shift_matrix()
    bias_rows = jnp.concatenate([bias_in[...], jnp.zeros((128 - LAYERS, HID), F32)], axis=0)
    bias_col[...] = bias_rows.T
    for copy in loaded:
        copy.wait()
    prepare(0)
    forward(0)
    output(0)
    halos[1].start()
    prepare(1)
    stretch_ahead()
    for layer in range(LAYERS):
        prepare_back(layer)
    by_rows(cot_in, cot_rows)
    for x in range(CX):
        flow[x] = cot_rows[x].astype(F32) * (1.0 / 256.0)
    forward(1)
    backward(1)
    backward_norm(1)
    halos[2].start()
    sums[1].start(grad_w.at[1])
    kernel_grad(windows.at[1], conv_grad, grad_k, 64, True)
    sums[1].to_plane()
    for x in range(CX):
        windows[1, MAIN + x] = conv_grad[x]
    halos[2].near(shifts, halo, windows.at[1])
    depthwise(windows.at[1], spread.at[1], conv, True, True)
    halos[2].far(shifts, halo, windows.at[1])
    depthwise(windows.at[1], spread.at[1], conv, True, False)
    for x in range(CX):
        flow[x] = flow[x] + conv[x]
    sums[1].to_line()
    backward(0)
    sums[0].start(grad_w.at[0])
    backward_norm(0)
    sums[1].back_line()
    kernel_grad(windows.at[0], conv_grad, grad_k, 0, False)
    sums[0].start_extra(grad_k)
    sums[0].to_plane()
    sums[0].to_line()
    sums[1].back_plane()
    sums[0].back_line()
    sums[0].back_plane()
    sums[1].back_twin()
    sums[0].back_twin()
    chosen = [jnp.zeros((C, 128), BF16), jnp.zeros((C, 128), BF16)]
    for which in range(LAYERS):
        for col in range(6):
            hit = block_at((C, 128)) == 6 * which + col
            for mat in range(2):
                tiles = [totals[(which, mat) + divmod(6 * row + col, SHARE)] for row in range(12)]
                chosen[mat] = jnp.where(hit, jnp.concatenate(tiles, axis=0), chosen[mat])
    grads = joined(chosen[0].astype(F32), chosen[1].astype(F32))
    cycle_out[...] = (ahead[...] + STEP_RATE * grads).astype(BF16)
    passed = remote(cycle_out, cycle_came, cycle_sem.at[0], cycle_sem.at[1], partner)
    passed.start()
    for each in halos + sums:
        each.close()
    passed.wait()


def whole_step(*operands):
    dma = pltpu.SemaphoreType.DMA
    vmem = pltpu.VMEM
    sums = ([dma((9,))] * 2 + [dma((7,))] * 8 + [dma((8,))] * 2) * LAYERS
    return pl.pallas_call(
        step_kernel,
        out_shape=[
            jax.ShapeDtypeStruct((LAYERS, 2, XY, SHARE + 1, 16, 128), BF16),
            jax.ShapeDtypeStruct((C, 128), BF16),
        ],
        in_specs=[pl.BlockSpec(memory_space=pltpu.SMEM)]
        + [pl.BlockSpec(memory_space=pltpu.VMEM)] * 9
        + [pl.BlockSpec(memory_space=pl.ANY)] * 4,
        out_specs=[pl.BlockSpec(memory_space=pltpu.VMEM)] * 2,
        scratch_shapes=[
            vmem((C * CX, CY), F32),
            vmem((CX, C, CY), BF16),
            vmem((CX, C, CY), BF16),
            vmem((2, LAYERS, C, HID), F32),
            vmem((2, LAYERS, C, HID), F32),
            vmem((C, 128), F32),
            vmem((128, 256), F32),
            vmem((LAYERS, C, 128), F32),
            vmem((HID, 128), F32),
            vmem((LAYERS, C, HID), BF16),
            vmem((LAYERS, HID, C), BF16),
            vmem((LAYERS, C, HID), BF16),
            vmem((LAYERS, HID, C), BF16),
            vmem((2 * CY, 6 * CY), BF16),
            vmem((LAYERS, 49, C, CY), F32),
            vmem((LAYERS, 7 * ROWS, C, CY), F32),
            vmem((ROWS, C, CY), BF16),
            vmem((CX, C, CY), F32),
            vmem((LAYERS, CX, C, CY), F32),
            vmem((LAYERS, CX, CY), F32),
            vmem((LAYERS, C, CELLS), BF16),
            vmem((HID, CELLS), F32),
            vmem((LAYERS, HID, CELLS), F32),
            vmem((LAYERS, HID, CELLS), BF16),
            vmem((CX, C, CY), F32),
            vmem((C, CELLS), BF16),
            vmem((HID, CELLS), BF16),
            vmem((CX, C, CY), F32),
            vmem((LAYERS, 2, C, HID), F32),
            vmem((C, 128), F32),
            vmem((2, CX, C, CY), BF16),
            vmem((3, FOLDED, CY), BF16),
            vmem((3, 2, 3, C, CY), BF16),
            vmem((3, 2, 3, FOLDED, CY), BF16),
            vmem((LAYERS, 80, 16, 128), BF16),
            vmem((LAYERS, 80, 16, 128), BF16),
            vmem((LAYERS, 80, 16, 128), F32),
            vmem((LAYERS, EW * ZT, 16, 128), F32),
            vmem((LAYERS, XY - 1, SHARE + 1, 16, 128), BF16),
            vmem((LAYERS, XY - 1, SHARE + 1, 16, 128), BF16),
            vmem((LAYERS, EW * ZT, 16, 128), BF16),
            vmem((LAYERS, EW - 1, ZT, 16, 128), BF16),
            vmem((LAYERS, EW * ZT, 16, 128), BF16),
            vmem((C, 128), BF16),
            dma((3, 8)),
            dma((3, 8)),
            dma((2,)),
            dma((2,)),
            dma((2,)),
        ]
        + sums,
        compiler_params=pltpu.CompilerParams(
            collective_id=0, has_side_effects=True, vmem_limit_bytes=60 * 2**20
        ),
    )(*operands)


def update_kernel(
    totals, stretch, win, wout_t, taps_in, new_in, new_out, new_k, cycle_in, cycle_out
):
    for layer in range(LAYERS):
        for tile in range(72):
            row, col = divmod(tile, 6)
            at = (layer, slice(16 * row, 16 * (row + 1)), slice(128 * col, 128 * (col + 1)))
            spot = divmod(tile, SHARE)
            new_in[at] = win[at] - STEP_RATE * totals[(layer, 0) + spot].astype(F32)
            new_out[at] = wout_t[at] - STEP_RATE * totals[(layer, 1) + spot].astype(F32)
    grads = [totals[0, half, tile, SHARE].astype(F32) for half in range(2) for tile in range(6)]
    taps = jnp.concatenate(grads, axis=0).T
    for layer in range(LAYERS):
        new_k[:, layer, :] = taps_in[:, layer, :] - STEP_RATE * taps[64 * layer : 64 * layer + 49]
    turned = stretch[...].astype(F32).T
    cycle_in[...] = turned[0:64]
    cycle_out[...] = turned[64:128]


def update(totals, stretch, win, wout_t, taps):
    weights = jax.ShapeDtypeStruct((LAYERS, C, HID), F32)
    part = jax.ShapeDtypeStruct((64, C), F32)
    return pl.pallas_call(
        update_kernel,
        out_shape=[weights, weights, jax.ShapeDtypeStruct((49, LAYERS, C), F32), part, part],
        in_specs=[pl.BlockSpec(memory_space=pltpu.VMEM)] * 5,
        out_specs=[pl.BlockSpec(memory_space=pltpu.VMEM)] * 5,
        compiler_params=pltpu.CompilerParams(vmem_limit_bytes=40 * 2**20),
    )(totals, stretch, win, wout_t, taps)


def body(
    fields,
    cotangent,
    land_mask,
    stretch_index,
    depth_kernel,
    norm_gain,
    norm_bias,
    weight_in,
    bias_in,
    weight_out,
    bias_out,
    layer_scale,
    anchor_in,
    anchor_out,
):
    win = weight_in[0]
    wout_t = weight_out[0].transpose(0, 2, 1)
    taps = depth_kernel[0].transpose(2, 0, 1)
    totals, stretch = whole_step(
        stretch_index,
        fields.reshape(C * CX, CY),
        cotangent.reshape(C * CX, CY),
        land_mask,
        taps,
        norm_gain[0],
        norm_bias[0],
        bias_out[0],
        layer_scale[0],
        bias_in[0],
        win,
        wout_t,
        anchor_in,
        anchor_out.transpose(0, 2, 1),
    )
    new_in, new_out, new_k, cycle_in, cycle_out = update(totals, stretch, win, wout_t, taps)
    return (
        new_k.transpose(1, 2, 0)[None],
        new_in[None],
        new_out.transpose(0, 2, 1)[None],
        cycle_in.T[None],
        cycle_out[None],
    )


def solution(mesh):
    in_specs = (
        P("rep", None, "ew", "ns"),
        P("rep", None, "ew", "ns"),
        P("ew", "ns"),
        P(),
        P("rep", None, None, None),
        P("rep", None, None),
        P("rep", None, None),
        P("rep", None, None, None),
        P("rep", None, None),
        P("rep", None, None, None),
        P("rep", None, None),
        P("rep", None, None),
        P(),
        P(),
    )
    out_specs = (
        P("rep", None, None, None),
        P("rep", None, None, None),
        P("rep", None, None, None),
        P("rep", None, None),
        P("rep", None, None),
    )
    return jax.shard_map(body, mesh=mesh, in_specs=in_specs, out_specs=out_specs, check_vma=False)
```

time: 119 us -> 90.7 us (0.76)
  Pallas kernels: 101 us -> 87 us
  local copies, waits for them, and re-layouts: 10.5 us -> 2.12 us
  waiting for transfers between devices: 3.45 us -> 0 us
  starting transfers between devices: 2.45 us -> 0 us
    pallas_call x1, Pallas kernels: 99.5 us -> 85.3 us  [whole_step(): pl.pallas_call(step_kernel, out_shape=[jax.ShapeDtypeStruct((LAYERS, 2, X...]
    ppermute x1 -> x0, waiting for transfers between devices: 3.45 us -> none  [body(): cycle = lax.ppermute(cycle, 'rep', [(0, 1), (1, 0)])]
    another operation x4 -> x0, local copies, waits for them, and re-layouts: 2.73 us -> none  [body(): jnp.stack([norm_gain[0], norm_bias[0], bias_out[0], layer_scale[0]], axis=1)]
    ppermute x1 -> x0, starting transfers between devices: 2.45 us -> none  [body(): cycle = lax.ppermute(cycle, 'rep', [(0, 1), (1, 0)])]
    pad x2 -> x0, local copies, waits for them, and re-layouts: 2.18 us -> none  [the longest x1 1.46 us: body(): bias = jnp.pad(bias_in[0], ((0, 128 - LAYERS), (0, 0)))]
    unnamed x18 -> x10, local copies, waits for them, and re-layouts: 4.06 us -> 2.12 us
  transfers between devices with their start and end apart: 1 -> 0, of which waited for: 1 -> 0; matrix products, arithmetic and copies ran while one was open for 1% -> 0% of each run, Pallas kernels for 0% -> 0%
where the time goes in v2:
time: 90.7 us; the launch traced here: 90.5 us
  Pallas kernels  87 us (96%)
  local copies, waits for them, and re-layouts  2.12 us (2%)
  between operations  1.35 us (1%)
    pallas_call x1, Pallas kernels, whole_step(): pl.pallas_call(step_kernel, out_shape=[jax.ShapeDtypeStruct((LAYERS, 2, X...  85.3 us
    unnamed x10, local copies, waits for them, and re-layouts  2.12 us

profile of v2, /device:TPU:1, one launch (start us, length us, event | category | flops | bytes accessed | tf_op | source)
XLA Modules:
  0.0 90.5 jit_solution(6042278316830099578)
XLA Ops:
  1.3 0.0 copy-start
  1.3 0.0 copy-start.1
  1.3 0.0 copy-start.3
  1.3 85.3 %shard_map.173 = (bf16[2,2,8,10,16,128]{5,4,3,2,1,0:T(8,128)(2,1)}, bf16[192,128]{1,0:T(8,128)(2,1)}) custom-call(s32[1]{0:T(128)S(6)} %copy.19.index, bf16[768,128]{1,0:T(8,128)(2,1)} %bitcast.33, bf16[768,128]{1,0:T(8,128)(2,1)} %bitcast.34, s32[4,128]{1,0:T(4,128)} %mask_in.1, f32[49,2,192]{2,1,0:T(2,128)} %bitcast.30, f32[2,192]{1,0:T(2,128)} %bitcast.36, ...), custom_call_target="tpu_custom_call" | custom-call | tf_op jit(solution)/shard_map/pallas_call | solution.py:714
  86.7 0.0 copy-done
  86.7 0.0 copy-done.1
  86.7 0.0 copy-done.3
  86.7 0.0 copy-start.2
  86.7 1.3 %copy-done.2 = bf16[2,2,8,10,16,128]{5,4,3,2,1,0:T(8,128)(2,1)S(1)} copy-done((bf16[2,2,8,10,16,128]{5,4,3,2,1,0:T(8,128)(2,1)S(1)}, bf16[2,2,8,10,16,128]{5,4,3,2,1,0:T(8,128)(2,1)}, u32[]{:S(2)}) %copy-start.2) | copy-done | bytes 1310744
  88.0 0.0 copy-start.4
  88.0 0.8 copy-done.4
  88.8 1.7 %shard_map.174 = (f32[2,192,768]{2,1,0:T(8,128)}, f32[2,192,768]{2,1,0:T(8,128)}, f32[49,2,192]{2,1,0:T(2,128)}, f32[64,192]{1,0:T(8,128)}, f32[64,192]{1,0:T(8,128)}) custom-call(bf16[2,2,8,10,16,128]{5,4,3,2,1,0:T(8,128)(2,1)S(1)} %copy-done.2, bf16[192,128]{1,0:T(8,128)(2,1)S(1)} %copy-done.4, f32[2,192,768]{2,1,0:T(8,128)S(1)} %bitcast.27, ...), custom_call_target="tpu_custom_call" | custom-call | tf_op jit(solution)/shard_map/pallas_call | solution.py:804
Async XLA Ops:
  1.3 85.4 %copy-start = (f32[1,2,192,768]{3,2,1,0:T(8,128)S(1)}, f32[1,2,192,768]{3,2,1,0:T(8,128)}, u32[]{:S(2)}) copy-start(f32[1,2,192,768]{3,2,1,0:T(8,128)} %param.21) | copy-start | bytes 3538948
  1.3 85.4 %copy-start.1 = (f32[1,2,768,192]{2,3,1,0:T(8,128)S(1)}, f32[1,2,768,192]{2,3,1,0:T(8,128)}, u32[]{:S(2)}) copy-start(f32[1,2,768,192]{2,3,1,0:T(8,128)} %param.23) | copy-start | bytes 3538948
  1.3 85.4 %copy-start.3 = (f32[1,2,192,49]{2,1,3,0:T(2,128)S(1)}, f32[1,2,192,49]{2,1,3,0:T(2,128)}, u32[]{:S(2)}) copy-start(f32[1,2,192,49]{2,1,3,0:T(2,128)} %param.18) | copy-start | bytes 225796
  86.7 1.3 %copy-start.2 = (bf16[2,2,8,10,16,128]{5,4,3,2,1,0:T(8,128)(2,1)S(1)}, bf16[2,2,8,10,16,128]{5,4,3,2,1,0:T(8,128)(2,1)}, u32[]{:S(2)}) copy-start(bf16[2,2,8,10,16,128]{5,4,3,2,1,0:T(8,128)(2,1)} %get-tuple-element.12.totals) | copy-start | bytes 3932164
  88.0 0.8 copy-start.4

commit v3 on v2

--- a/solution.py
+++ b/solution.py
@@ -22,6 +22,8 @@
 ROWS = CX + 6
 BLOCKS = C // 8
 FOLD = 4
+CUTS = 3
+CUT = C // CUTS
 FOLDED = C // FOLD
 XY = 8
 EW = 8
@@ -97,18 +99,22 @@
         self.row_copies = []
         self.edge_copies = []
 
-    def start(self):
-        place = self.place
+    def send_rows(self, cut):
+        at = pl.ds(CUT * cut, CUT)
         for number, (first, step) in enumerate(((1, 1), (0, -1))):
             copy = remote(
-                self.rows.at[pl.ds(first, 3)],
-                self.in_rows.at[number],
-                self.sent.at[number],
-                self.came.at[number],
-                place.beside(step, 0),
+                self.rows.at[pl.ds(first, 3), at],
+                self.in_rows.at[number, :, at],
+                self.sent.at[2 * cut + number],
+                self.came.at[2 * cut + number],
+                self.place.beside(step, 0),
             )
             copy.start()
             self.row_copies.append(copy)
+
+    def start(self):
+        place = self.place
+        self.send_rows(0)
         slot = ((lanes_of((FOLDED, CY)) + 4) % CY) // 8
         folded = jnp.zeros((FOLDED, CY), F32)
         for x in range(CX):
@@ -124,12 +130,14 @@
             copy = remote(
                 self.out_edges,
                 self.in_edges.at[side, 1 - dz],
-                self.sent.at[2 + number],
-                self.came.at[2 + number],
+                self.sent.at[2 * CUTS + number],
+                self.came.at[2 * CUTS + number],
                 place.beside(dz, dn),
             )
             copy.start()
             self.edge_copies.append(copy)
+        for cut in range(1, CUTS):
+            self.send_rows(cut)
 
     def near(self, shifts, halo, windows):
         for copy in self.edge_copies:
@@ -152,30 +160,34 @@
                     moved = pltpu.roll(edges, CY - 8 * number, 1) if number else edges
                     halo[row, FOLDED * part : FOLDED * (part + 1), :] = moved.astype(BF16)
 
-        self.shift(self.rows, 3, CX, shifts, halo, windows)
-
-    def shift(self, rows, first, count, shifts, halo, windows):
         cells = jnp.concatenate(
-            [
-                rows[...].reshape(count * C, CY),
-                halo[first : first + count].reshape(count * C, CY),
-            ],
-            axis=1,
+            [self.rows[...].reshape(CX * C, CY), halo[3 : 3 + CX].reshape(CX * C, CY)], axis=1
         )
         moved = dot(cells, shifts[...])
         for place, col in enumerate(SHIFTED):
-            start = col * ROWS + first
-            windows[start : start + count] = moved[:, CY * place : CY * (place + 1)].reshape(
-                count, C, CY
+            start = col * ROWS + 3
+            part = moved[:, CY * place : CY * (place + 1)]
+            windows[start : start + CX] = part.reshape(CX, C, CY)
+
+    def far(self, shifts, halo, windows, cut):
+        for copy in self.row_copies[2 * cut : 2 * cut + 2]:
+            copy.wait_recv()
+        at = slice(CUT * cut, CUT * (cut + 1))
+        cells = []
+        for side, first in ((0, 0), (1, CX + 3)):
+            rows = self.in_rows[side, :, at]
+            rims = halo[first : first + 3, at]
+            cells.append(
+                jnp.concatenate([rows.reshape(3 * CUT, CY), rims.reshape(3 * CUT, CY)], axis=1)
             )
-
-    def far(self, shifts, halo, windows):
-        for copy in self.row_copies:
-            copy.wait_recv()
+            start = 3 * ROWS + first
+            windows[start : start + 3, at] = rows.astype(F32)
+        moved = dot(jnp.concatenate(cells, axis=0), shifts[...])
         for side, first in ((0, 0), (1, CX + 3)):
-            self.shift(self.in_rows.at[side], first, 3, shifts, halo, windows)
-            start = 3 * ROWS + first
-            windows[start : start + 3] = self.in_rows[side].astype(F32)
+            for place, col in enumerate(SHIFTED):
+                start = col * ROWS + first
+                part = moved[3 * CUT * side : 3 * CUT * (side + 1), CY * place : CY * (place + 1)]
+                windows[start : start + 3, at] = part.reshape(3, CUT, CY)
 
     def close(self):
         for copy in self.row_copies + self.edge_copies:
@@ -193,17 +205,28 @@
     return jnp.concatenate(parts, axis=1)
 
 
-def spread_taps(taps, out):
-    @pl.loop(0, BLOCKS, unroll=4)
-    def _(block):
-        at = pl.ds(block * 8, 8)
-        weights = taps[at, :]
-        for tap in range(49):
-            out[tap, at, :] = jnp.broadcast_to(weights[:, tap : tap + 1], (8, CY))
-
-
-def depthwise(windows, spread, out, reverse, own):
-    @pl.loop(0, BLOCKS, unroll=2)
+def spread_taps(cols, out):
+    parts = []
+    for layer in range(LAYERS):
+        taps = cols[layer]
+        high = taps.astype(BF16).astype(F32)
+        middle = (taps - high).astype(BF16).astype(F32)
+        parts.append(
+            jnp.concatenate([high + pltpu.roll(middle, 64, 1), taps - high - middle], axis=1)
+        )
+    left = jnp.concatenate(parts, axis=0).astype(BF16)
+    source = lax.broadcasted_iota(jnp.int32, (256, 128), 0) % 64
+    for tap in range(0, 50, 2):
+        picks = [(source == tap + side).astype(F32).astype(BF16) for side in range(2)]
+        moved = dot(left, jnp.concatenate(picks, axis=1))
+        for layer in range(LAYERS):
+            rows = slice(C * layer, C * (layer + 1))
+            out[layer, tap] = moved[rows, 0:CY]
+            out[layer, tap + 1] = moved[rows, CY : 2 * CY]
+
+
+def depthwise(windows, spread, out, reverse, own, first=0, blocks=BLOCKS):
+    @pl.loop(first, first + blocks, unroll=4)
     def _(block):
         at = pl.ds(block * 8, 8)
         total = [None if own else out[x, at, :] for x in range(CX)]
@@ -228,7 +251,7 @@
 
 
 def kernel_grad(windows, conv_grad, out, lane_base, first):
-    @pl.loop(0, BLOCKS, unroll=4)
+    @pl.loop(0, BLOCKS, unroll=8)
     def _(block):
         at = pl.ds(block * 8, 8)
         lane = lanes_of((8, CY))
@@ -314,27 +337,35 @@
 
     def to_plane(self):
         self.second = []
-        if self.extra is not None:
-            self.extra.wait_recv()
         self.mine[...] = jnp.zeros_like(self.mine)
         for step, copy in self.first:
             copy.wait_recv()
             part = self.own[self.share(step)] + self.recv1[self.share(step)].astype(F32)
-            if self.extra is not None:
-                spot = 72 + self.chunk(step)
-                more = self.own[spot] + self.recv1[spot].astype(F32)
             if step == 0:
                 self.mine[0:SHARE] = part
-                if self.extra is not None:
-                    self.mine[SHARE] = more
             else:
                 self.send2[step - 1, 0:SHARE] = part.astype(BF16)
-                if self.extra is not None:
-                    self.send2[step - 1, SHARE] = more.astype(BF16)
                 copy = remote(
-                    self.send2.at[step - 1, pl.ds(0, self.tiles)],
-                    self.recv2.at[step - 1, pl.ds(0, self.tiles)],
+                    self.send2.at[step - 1, pl.ds(0, SHARE)],
+                    self.recv2.at[step - 1, pl.ds(0, SHARE)],
                     *self.pair(1, step - 1),
+                    self.place.in_plane(step),
+                )
+                self.second.append(self.go(copy))
+
+    def extra_to_plane(self):
+        self.extra.wait_recv()
+        for step in list(range(1, XY)) + [0]:
+            spot = 72 + self.chunk(step)
+            part = self.own[spot] + self.recv1[spot].astype(F32)
+            if step == 0:
+                self.mine[SHARE] = part
+            else:
+                self.send2[step - 1, SHARE] = part.astype(BF16)
+                copy = remote(
+                    self.send2.at[step - 1, pl.ds(SHARE, 1)],
+                    self.recv2.at[step - 1, pl.ds(SHARE, 1)],
+                    *self.pair(6, step - 1),
                     self.place.in_plane(step),
                 )
                 self.second.append(self.go(copy))
@@ -387,6 +418,10 @@
         mine[...] = share[...]
 
     def back_twin(self):
+        self.forward_twin()
+        self.end_twin()
+
+    def forward_twin(self):
         for step, copy in enumerate(self.fifth):
             copy.wait_recv()
             came = self.total.at[
@@ -396,6 +431,8 @@
             ]
             copy = remote(came, came, *self.pair(5, step + 1), self.place.twin())
             self.sixth.append(self.go(copy))
+
+    def end_twin(self):
         for copy in self.sixth:
             copy.wait_recv()
 
@@ -420,7 +457,6 @@
     anchor_in,
     anchor_out,
     totals,
-    cycle_came,
     cells_t,
     x_rows,
     cot_rows,
@@ -464,18 +500,25 @@
     send3,
     recv3,
     line,
-    cycle_out,
+    picks,
+    came,
+    tiles_by,
+    ahead_came,
     halo_sent,
     halo_came,
     weight_sem,
     anchor_sem,
-    cycle_sem,
+    ahead_sem,
+    tiles_sem,
+    pick_sent,
+    pick_came,
     *sems,
 ):
     place = Place()
     barrier = pltpu.get_barrier_semaphore()
     partner = (1 - place.rep, place.z, place.ns)
-    peers = [place.twin(), partner]
+    peers = [place.twin()]
+    peers += [(1 - place.rep,) + place.in_plane(d)[1:] for d in range(XY)]
     peers += [place.in_plane(d) for d in range(1, XY)]
     peers += [place.on_line(d) for d in range(1, EW)]
     peers += [place.beside(dz, dn) for dz, dn in AROUND]
@@ -523,12 +566,12 @@
             recv3.at[layer],
             line.at[layer],
             totals.at[layer],
-            sems[12 * layer : 12 * (layer + 1)],
+            sems[14 * layer : 14 * (layer + 1)],
         )
         for layer in range(LAYERS)
     ]
 
-    def prepare(layer):
+    def columns(layer):
         rows_t[...] = jnp.zeros_like(rows_t)
         rows_t[0:49, 0:C] = taps_in[:, layer, :]
         for row, vector in (
@@ -539,9 +582,10 @@
         ):
             rows_t[row : row + 1, 0:C] = vector[layer : layer + 1, :]
         cols[layer] = rows_t[...].T[:C]
+
+    def prepare(layer):
         win_tb[layer] = win[layer].T.astype(BF16)
         wout_tb[layer] = wout_t[layer].astype(BF16)
-        spread_taps(cols.at[layer], spread.at[layer])
 
     def prepare_back(layer):
         win_b[layer] = win[layer].astype(BF16)
@@ -552,11 +596,16 @@
     def column(layer, which):
         return cols[layer, :, which : which + 1]
 
+    def outer(turn, layer, reverse):
+        for cut in range(CUTS):
+            halos[turn].far(shifts, halo, windows.at[layer], cut)
+            part = (cut * (CUT // 8), CUT // 8)
+            depthwise(windows.at[layer], spread.at[layer], conv, reverse, False, *part)
+
     def forward(layer):
         halos[layer].near(shifts, halo, windows.at[layer])
         depthwise(windows.at[layer], spread.at[layer], conv, False, True)
-        halos[layer].far(shifts, halo, windows.at[layer])
-        depthwise(windows.at[layer], spread.at[layer], conv, False, False)
+        outer(layer, layer, False)
         for x in range(CX):
             cells = conv[x]
             centered = cells - jnp.mean(cells, axis=0, keepdims=True)
@@ -569,7 +618,7 @@
             ).astype(BF16)
         hidden[...] = dot(win_tb[layer], norm_b[layer])
 
-        @pl.loop(0, HID // 192)
+        @pl.loop(0, HID // 192, unroll=4)
         def _(block):
             at = pl.ds(block * 192, 192)
             pre = hidden[at, :] + bias_col[at, layer : layer + 1]
@@ -596,7 +645,7 @@
         grad_w[layer, 1] = dot_cells(back_b[...], act_b[layer])
         hidden[...] = dot(wout_b[layer], back_b[...])
 
-        @pl.loop(0, HID // 192)
+        @pl.loop(0, HID // 192, unroll=4)
         def _(block):
             at = pl.ds(block * 192, 192)
             hid_b[at, :] = (hidden[at, :] * slope[layer, at, :]).astype(BF16)
@@ -620,8 +669,11 @@
         for x in range(CX):
             out[x] = cells_t[pl.ds(x, C, stride=CX), :].astype(BF16)
 
-    def block_at(shape):
-        return jnp.full(shape, index[0] // 2, jnp.int32)
+    def hits(shape):
+        spot = jnp.full(shape, index[0] // 2, jnp.int32)
+        return [
+            (layer, col, spot == 6 * layer + col) for layer in range(LAYERS) for col in range(6)
+        ]
 
     def joined(first, second):
         odd = jnp.full((C, 128), lax.rem(index[0], 2), jnp.int32) == 1
@@ -633,13 +685,63 @@
         for copy in fetched:
             copy.wait()
         chosen = [jnp.zeros((C, 128), F32), jnp.zeros((C, 128), F32)]
-        for which in range(LAYERS):
-            for col in range(6):
-                hit = block_at((C, 128)) == 6 * which + col
-                for mat, weights in enumerate((win, wout_t)):
-                    at = (which, slice(0, C), slice(128 * col, 128 * (col + 1)))
-                    chosen[mat] = jnp.where(hit, anchors[(mat,) + at] - weights[at], chosen[mat])
+        for layer, col, hit in hits((C, 128)):
+            at = (layer, slice(0, C), slice(128 * col, 128 * (col + 1)))
+            for mat, weights in enumerate((win, wout_t)):
+                chosen[mat] = jnp.where(hit, anchors[(mat,) + at] - weights[at], chosen[mat])
         ahead[...] = joined(*chosen)
+        copy = remote(ahead, ahead_came, ahead_sem.at[0], ahead_sem.at[1], partner)
+        copy.start()
+        return copy
+
+    def stretch_share():
+        for slot in range(2):
+            picked = jnp.zeros((16, 128), BF16)
+            for layer, col, hit in hits((16, 128)):
+                at = lax.rem(col + 3 * place.chip, 6) + 6 * slot
+                picked = jnp.where(hit, line[layer, at], picked)
+            picks[slot] = picked
+        copies = []
+        for step in range(XY):
+            z, ns = place.in_plane(step)[1:]
+            copies.append(
+                remote(
+                    picks, came.at[step], pick_sent.at[step], pick_came.at[step], (1 - place.rep, z, ns)
+                )
+            )
+        for copy in copies:
+            copy.start()
+        return copies
+
+    def stretch_gather(copies):
+        for step, copy in enumerate(copies):
+            copy.wait_recv()
+            source = lax.rem(place.chip + XY - step, XY)
+            tiles_by[place.core, source] = came[step]
+        part = tiles_by.at[place.core]
+        copy = remote(part, part, tiles_sem.at[0], tiles_sem.at[1], place.twin())
+        copy.start()
+        return copy
+
+    def stretch_result():
+        chosen = [jnp.zeros((C, 128), BF16), jnp.zeros((C, 128), BF16)]
+        spot = lax.rem(jnp.full((C, 128), index[0] // 2, jnp.int32), 6)
+        for col in range(6):
+            for mat in range(2):
+                rows = []
+                for row in range(12):
+                    chip, inside = divmod(6 * row + col, SHARE)
+                    rows.append(tiles_by[mat, chip, inside // 6])
+                rows = jnp.concatenate(rows, axis=0)
+                chosen[mat] = jnp.where(spot == col, rows, chosen[mat])
+        grads = joined(chosen[0].astype(F32), chosen[1].astype(F32))
+        result = (ahead_came[...] + STEP_RATE * grads).astype(BF16)
+        for row in range(12):
+            spot = (1,) + divmod(row, XY) + (SHARE,)
+            totals[spot] = result[16 * row : 16 * (row + 1), :]
+        for row in range(12, 16):
+            totals[(1,) + divmod(row, XY) + (SHARE,)] = jnp.zeros((16, 128), BF16)
+
 
     by_rows(x_in, x_rows)
     pl.semaphore_wait(barrier, len(peers))
@@ -649,6 +751,9 @@
     shifts[...] = shift_matrix()
     bias_rows = jnp.concatenate([bias_in[...], jnp.zeros((128 - LAYERS, HID), F32)], axis=0)
     bias_col[...] = bias_rows.T
+    for layer in range(LAYERS):
+        columns(layer)
+    spread_taps(cols, spread)
     for copy in loaded:
         copy.wait()
     prepare(0)
@@ -656,7 +761,6 @@
     output(0)
     halos[1].start()
     prepare(1)
-    stretch_ahead()
     for layer in range(LAYERS):
         prepare_back(layer)
     by_rows(cot_in, cot_rows)
@@ -668,59 +772,53 @@
     halos[2].start()
     sums[1].start(grad_w.at[1])
     kernel_grad(windows.at[1], conv_grad, grad_k, 64, True)
+    passed = stretch_ahead()
     sums[1].to_plane()
     for x in range(CX):
         windows[1, MAIN + x] = conv_grad[x]
     halos[2].near(shifts, halo, windows.at[1])
     depthwise(windows.at[1], spread.at[1], conv, True, True)
-    halos[2].far(shifts, halo, windows.at[1])
-    depthwise(windows.at[1], spread.at[1], conv, True, False)
+    outer(2, 1, True)
     for x in range(CX):
         flow[x] = flow[x] + conv[x]
     sums[1].to_line()
     backward(0)
     sums[0].start(grad_w.at[0])
     backward_norm(0)
+    sums[0].to_plane()
     sums[1].back_line()
     kernel_grad(windows.at[0], conv_grad, grad_k, 0, False)
     sums[0].start_extra(grad_k)
-    sums[0].to_plane()
+    sums[0].extra_to_plane()
     sums[0].to_line()
     sums[1].back_plane()
     sums[0].back_line()
     sums[0].back_plane()
+    picked = stretch_share()
     sums[1].back_twin()
-    sums[0].back_twin()
-    chosen = [jnp.zeros((C, 128), BF16), jnp.zeros((C, 128), BF16)]
-    for which in range(LAYERS):
-        for col in range(6):
-            hit = block_at((C, 128)) == 6 * which + col
-            for mat in range(2):
-                tiles = [totals[(which, mat) + divmod(6 * row + col, SHARE)] for row in range(12)]
-                chosen[mat] = jnp.where(hit, jnp.concatenate(tiles, axis=0), chosen[mat])
-    grads = joined(chosen[0].astype(F32), chosen[1].astype(F32))
-    cycle_out[...] = (ahead[...] + STEP_RATE * grads).astype(BF16)
-    passed = remote(cycle_out, cycle_came, cycle_sem.at[0], cycle_sem.at[1], partner)
-    passed.start()
+    sums[0].forward_twin()
+    joined_copy = stretch_gather(picked)
+    sums[0].end_twin()
+    passed.wait()
+    joined_copy.wait()
+    stretch_result()
+    for copy in picked:
+        copy.wait_send()
     for each in halos + sums:
         each.close()
-    passed.wait()
 
 
 def whole_step(*operands):
     dma = pltpu.SemaphoreType.DMA
     vmem = pltpu.VMEM
-    sums = ([dma((9,))] * 2 + [dma((7,))] * 8 + [dma((8,))] * 2) * LAYERS
+    sums = ([dma((9,))] * 2 + [dma((7,))] * 8 + [dma((8,))] * 2 + [dma((7,))] * 2) * LAYERS
     return pl.pallas_call(
         step_kernel,
-        out_shape=[
-            jax.ShapeDtypeStruct((LAYERS, 2, XY, SHARE + 1, 16, 128), BF16),
-            jax.ShapeDtypeStruct((C, 128), BF16),
-        ],
+        out_shape=jax.ShapeDtypeStruct((LAYERS, 2, XY, SHARE + 1, 16, 128), BF16),
         in_specs=[pl.BlockSpec(memory_space=pltpu.SMEM)]
         + [pl.BlockSpec(memory_space=pltpu.VMEM)] * 9
         + [pl.BlockSpec(memory_space=pl.ANY)] * 4,
-        out_specs=[pl.BlockSpec(memory_space=pltpu.VMEM)] * 2,
+        out_specs=pl.BlockSpec(memory_space=pltpu.VMEM),
         scratch_shapes=[
             vmem((C * CX, CY), F32),
             vmem((CX, C, CY), BF16),
@@ -736,7 +834,7 @@
             vmem((LAYERS, C, HID), BF16),
             vmem((LAYERS, HID, C), BF16),
             vmem((2 * CY, 6 * CY), BF16),
-            vmem((LAYERS, 49, C, CY), F32),
+            vmem((LAYERS, 50, C, CY), F32),
             vmem((LAYERS, 7 * ROWS, C, CY), F32),
             vmem((ROWS, C, CY), BF16),
             vmem((CX, C, CY), F32),
@@ -765,12 +863,18 @@
             vmem((LAYERS, EW * ZT, 16, 128), BF16),
             vmem((LAYERS, EW - 1, ZT, 16, 128), BF16),
             vmem((LAYERS, EW * ZT, 16, 128), BF16),
-            vmem((C, 128), BF16),
-            dma((3, 8)),
-            dma((3, 8)),
+            vmem((2, 16, 128), BF16),
+            vmem((XY, 2, 16, 128), BF16),
+            vmem((2, XY, 2, 16, 128), BF16),
+            vmem((C, 128), F32),
+            dma((3, 2 * CUTS + 6)),
+            dma((3, 2 * CUTS + 6)),
             dma((2,)),
             dma((2,)),
             dma((2,)),
+            dma((2,)),
+            dma((8,)),
+            dma((8,)),
         ]
         + sums,
         compiler_params=pltpu.CompilerParams(
@@ -780,7 +884,7 @@
 
 
 def update_kernel(
-    totals, stretch, win, wout_t, taps_in, new_in, new_out, new_k, cycle_in, cycle_out
+    totals, win, wout_t, taps_in, new_in, new_out, new_k, cycle_in, cycle_out
 ):
     for layer in range(LAYERS):
         for tile in range(72):
@@ -793,21 +897,22 @@
     taps = jnp.concatenate(grads, axis=0).T
     for layer in range(LAYERS):
         new_k[:, layer, :] = taps_in[:, layer, :] - STEP_RATE * taps[64 * layer : 64 * layer + 49]
-    turned = stretch[...].astype(F32).T
+    rows = [totals[(1,) + divmod(row, XY) + (SHARE,)].astype(F32) for row in range(12)]
+    turned = jnp.concatenate(rows, axis=0).T
     cycle_in[...] = turned[0:64]
     cycle_out[...] = turned[64:128]
 
 
-def update(totals, stretch, win, wout_t, taps):
+def update(totals, win, wout_t, taps):
     weights = jax.ShapeDtypeStruct((LAYERS, C, HID), F32)
     part = jax.ShapeDtypeStruct((64, C), F32)
     return pl.pallas_call(
         update_kernel,
         out_shape=[weights, weights, jax.ShapeDtypeStruct((49, LAYERS, C), F32), part, part],
-        in_specs=[pl.BlockSpec(memory_space=pltpu.VMEM)] * 5,
+        in_specs=[pl.BlockSpec(memory_space=pltpu.VMEM)] * 4,
         out_specs=[pl.BlockSpec(memory_space=pltpu.VMEM)] * 5,
         compiler_params=pltpu.CompilerParams(vmem_limit_bytes=40 * 2**20),
-    )(totals, stretch, win, wout_t, taps)
+    )(totals, win, wout_t, taps)
 
 
 def body(
@@ -829,7 +934,7 @@
     win = weight_in[0]
     wout_t = weight_out[0].transpose(0, 2, 1)
     taps = depth_kernel[0].transpose(2, 0, 1)
-    totals, stretch = whole_step(
+    totals = whole_step(
         stretch_index,
         fields.reshape(C * CX, CY),
         cotangent.reshape(C * CX, CY),
@@ -845,7 +950,7 @@
         anchor_in,
         anchor_out.transpose(0, 2, 1),
     )
-    new_in, new_out, new_k, cycle_in, cycle_out = update(totals, stretch, win, wout_t, taps)
+    new_in, new_out, new_k, cycle_in, cycle_out = update(totals, win, wout_t, taps)
     return (
         new_k.transpose(1, 2, 0)[None],
         new_in[None],

time: 90.7 us -> 80.4 us (0.89)
  Pallas kernels: 87 us -> 77.6 us
    pallas_call x1, Pallas kernels: 85.3 us -> 75.9 us  [whole_step(): pl.pallas_call(step_kernel, out_shape=jax.ShapeDtypeStruct((LAYERS, 2, XY...]
    unnamed x10 -> x8, local copies, waits for them, and re-layouts: 2.12 us -> 1.32 us
where the time goes in v3:
time: 80.4 us; the launch traced here: 80.2 us
  Pallas kernels  77.6 us (97%)
  between operations  1.35 us (2%)
  local copies, waits for them, and re-layouts  1.32 us (2%)
    pallas_call x1, Pallas kernels, whole_step(): pl.pallas_call(step_kernel, out_shape=jax.ShapeDtypeStruct((LAYERS, 2, XY...  75.9 us
    pallas_call x1, Pallas kernels, update(): pl.pallas_call(update_kernel, out_shape=[weights, weights, jax.ShapeDtype...  1.71 us

profile of v3, /device:TPU:1, one launch (start us, length us, event | category | flops | bytes accessed | tf_op | source)
XLA Modules:
  0.0 80.2 jit_solution(11263712351903071533)
XLA Ops:
  1.3 0.0 copy-start.1
  1.3 0.0 copy-start.2
  1.3 0.0 copy-start.3
  1.3 75.9 %shard_map.173.totals = bf16[2,2,8,10,16,128]{5,4,3,2,1,0:T(8,128)(2,1)} custom-call(s32[1]{0:T(128)S(6)} %copy.19.index, bf16[768,128]{1,0:T(8,128)(2,1)} %bitcast.33, bf16[768,128]{1,0:T(8,128)(2,1)} %bitcast.34, s32[4,128]{1,0:T(4,128)} %mask_in.1, f32[49,2,192]{2,1,0:T(2,128)} %bitcast.30, f32[2,192]{1,0:T(2,128)} %bitcast.36, f32[2,192]{1,0:T(2,128)} %bitcast.37, ...), custom_call_target="tpu_custom_call" | custom-call | tf_op jit(solution)/shard_map/pallas_call | solution.py:815
  77.2 0.0 copy-done.1
  77.2 0.0 copy-done.2
  77.2 0.0 copy-done.3
  77.2 0.0 copy-start
  77.2 1.3 %copy-done = bf16[2,2,8,10,16,128]{5,4,3,2,1,0:T(8,128)(2,1)S(1)} copy-done((bf16[2,2,8,10,16,128]{5,4,3,2,1,0:T(8,128)(2,1)S(1)}, bf16[2,2,8,10,16,128]{5,4,3,2,1,0:T(8,128)(2,1)}, u32[]{:S(2)}) %copy-start) | copy-done | bytes 1310744
  78.5 1.7 %shard_map.174 = (f32[2,192,768]{2,1,0:T(8,128)}, f32[2,192,768]{2,1,0:T(8,128)}, f32[49,2,192]{2,1,0:T(2,128)}, f32[64,192]{1,0:T(8,128)}, f32[64,192]{1,0:T(8,128)}) custom-call(bf16[2,2,8,10,16,128]{5,4,3,2,1,0:T(8,128)(2,1)S(1)} %copy-done, f32[2,192,768]{2,1,0:T(8,128)S(1)} %bitcast.27, f32[2,192,768]{2,1,0:T(8,128)S(1)} %bitcast.29, ...), custom_call_target="tpu_custom_call" | custom-call | tf_op jit(solution)/shard_map/pallas_call | solution.py:909
Async XLA Ops:
  1.3 75.9 %copy-start.1 = (f32[1,2,192,768]{3,2,1,0:T(8,128)S(1)}, f32[1,2,192,768]{3,2,1,0:T(8,128)}, u32[]{:S(2)}) copy-start(f32[1,2,192,768]{3,2,1,0:T(8,128)} %param.21) | copy-start | bytes 3538948
  1.3 75.9 %copy-start.2 = (f32[1,2,768,192]{2,3,1,0:T(8,128)S(1)}, f32[1,2,768,192]{2,3,1,0:T(8,128)}, u32[]{:S(2)}) copy-start(f32[1,2,768,192]{2,3,1,0:T(8,128)} %param.23) | copy-start | bytes 3538948
  1.3 75.9 %copy-start.3 = (f32[1,2,192,49]{2,1,3,0:T(2,128)S(1)}, f32[1,2,192,49]{2,1,3,0:T(2,128)}, u32[]{:S(2)}) copy-start(f32[1,2,192,49]{2,1,3,0:T(2,128)} %param.18) | copy-start | bytes 225796
  77.2 1.3 %copy-start = (bf16[2,2,8,10,16,128]{5,4,3,2,1,0:T(8,128)(2,1)S(1)}, bf16[2,2,8,10,16,128]{5,4,3,2,1,0:T(8,128)(2,1)}, u32[]{:S(2)}) copy-start(bf16[2,2,8,10,16,128]{5,4,3,2,1,0:T(8,128)(2,1)} %shard_map.173.totals) | copy-start | bytes 3932164

commit v4 on v3

--- a/solution.py
+++ b/solution.py
@@ -22,7 +22,7 @@
 ROWS = CX + 6
 BLOCKS = C // 8
 FOLD = 4
-CUTS = 3
+CUTS = 6
 CUT = C // CUTS
 FOLDED = C // FOLD
 XY = 8
@@ -114,7 +114,6 @@
 
     def start(self):
         place = self.place
-        self.send_rows(0)
         slot = ((lanes_of((FOLDED, CY)) + 4) % CY) // 8
         folded = jnp.zeros((FOLDED, CY), F32)
         for x in range(CX):
@@ -136,16 +135,28 @@
             )
             copy.start()
             self.edge_copies.append(copy)
-        for cut in range(1, CUTS):
+        for cut in range(CUTS):
             self.send_rows(cut)
 
     def near(self, shifts, halo, windows):
-        for copy in self.edge_copies:
-            copy.wait_recv()
+        self.rims(halo, (1,))
+        cells = jnp.concatenate(
+            [self.rows[...].reshape(CX * C, CY), halo[3 : 3 + CX].reshape(CX * C, CY)], axis=1
+        )
+        moved = dot(cells, shifts[...])
+        for place, col in enumerate(SHIFTED):
+            start = col * ROWS + 3
+            part = moved[:, CY * place : CY * (place + 1)]
+            windows[start : start + CX] = part.reshape(CX, C, CY)
+
+    def rims(self, halo, indices):
+        for copy, (dz, _) in zip(self.edge_copies, AROUND):
+            if 1 - dz in indices:
+                copy.wait_recv()
         keep_left = (self.place.ns > 0).astype(F32)
         keep_right = (self.place.ns < NS - 1).astype(F32)
         low = (lanes_of((FOLDED, CY)) + 4) % 8 < 4
-        for index in range(3):
+        for index in indices:
             edges = jnp.where(
                 low,
                 self.in_edges[0, index].astype(F32) * keep_left,
@@ -159,15 +170,6 @@
                     number = 4 * part + x
                     moved = pltpu.roll(edges, CY - 8 * number, 1) if number else edges
                     halo[row, FOLDED * part : FOLDED * (part + 1), :] = moved.astype(BF16)
-
-        cells = jnp.concatenate(
-            [self.rows[...].reshape(CX * C, CY), halo[3 : 3 + CX].reshape(CX * C, CY)], axis=1
-        )
-        moved = dot(cells, shifts[...])
-        for place, col in enumerate(SHIFTED):
-            start = col * ROWS + 3
-            part = moved[:, CY * place : CY * (place + 1)]
-            windows[start : start + CX] = part.reshape(CX, C, CY)
 
     def far(self, shifts, halo, windows, cut):
         for copy in self.row_copies[2 * cut : 2 * cut + 2]:
@@ -597,6 +599,7 @@
         return cols[layer, :, which : which + 1]
 
     def outer(turn, layer, reverse):
+        halos[turn].rims(halo, (0, 2))
         for cut in range(CUTS):
             halos[turn].far(shifts, halo, windows.at[layer], cut)
             part = (cut * (CUT // 8), CUT // 8)

time: 80.4 us -> 76.3 us (0.949)
  Pallas kernels: 77.6 us -> 73.5 us
    pallas_call x1, Pallas kernels: 75.9 us -> 71.8 us  [whole_step(): pl.pallas_call(step_kernel, out_shape=jax.ShapeDtypeStruct((LAYERS, 2, XY...]
where the time goes in v4:
time: 76.3 us; the launch traced here: 76.2 us
  Pallas kernels  73.5 us (96%)
  between operations  1.35 us (2%)
  local copies, waits for them, and re-layouts  1.32 us (2%)
    pallas_call x1, Pallas kernels, whole_step(): pl.pallas_call(step_kernel, out_shape=jax.ShapeDtypeStruct((LAYERS, 2, XY...  71.8 us
    pallas_call x1, Pallas kernels, update(): pl.pallas_call(update_kernel, out_shape=[weights, weights, jax.ShapeDtype...  1.71 us

profile of v4, /device:TPU:1, one launch (start us, length us, event | category | flops | bytes accessed | tf_op | source)
XLA Modules:
  0.0 76.2 jit_solution(7814029557623800586)
XLA Ops:
  1.3 0.0 copy-start.1
  1.3 0.0 copy-start.2
  1.3 0.0 copy-start.3
  1.3 71.8 %shard_map.173.totals = bf16[2,2,8,10,16,128]{5,4,3,2,1,0:T(8,128)(2,1)} custom-call(s32[1]{0:T(128)S(6)} %copy.19.index, bf16[768,128]{1,0:T(8,128)(2,1)} %bitcast.33, bf16[768,128]{1,0:T(8,128)(2,1)} %bitcast.34, s32[4,128]{1,0:T(4,128)} %mask_in.1, f32[49,2,192]{2,1,0:T(2,128)} %bitcast.30, f32[2,192]{1,0:T(2,128)} %bitcast.36, f32[2,192]{1,0:T(2,128)} %bitcast.37, ...), custom_call_target="tpu_custom_call" | custom-call | tf_op jit(solution)/shard_map/pallas_call | solution.py:818
  73.1 0.0 copy-done.1
  73.1 0.0 copy-done.2
  73.1 0.0 copy-done.3
  73.1 0.0 copy-start
  73.1 1.3 %copy-done = bf16[2,2,8,10,16,128]{5,4,3,2,1,0:T(8,128)(2,1)S(1)} copy-done((bf16[2,2,8,10,16,128]{5,4,3,2,1,0:T(8,128)(2,1)S(1)}, bf16[2,2,8,10,16,128]{5,4,3,2,1,0:T(8,128)(2,1)}, u32[]{:S(2)}) %copy-start) | copy-done | bytes 1310744
  74.4 1.7 %shard_map.174 = (f32[2,192,768]{2,1,0:T(8,128)}, f32[2,192,768]{2,1,0:T(8,128)}, f32[49,2,192]{2,1,0:T(2,128)}, f32[64,192]{1,0:T(8,128)}, f32[64,192]{1,0:T(8,128)}) custom-call(bf16[2,2,8,10,16,128]{5,4,3,2,1,0:T(8,128)(2,1)S(1)} %copy-done, f32[2,192,768]{2,1,0:T(8,128)S(1)} %bitcast.27, f32[2,192,768]{2,1,0:T(8,128)S(1)} %bitcast.29, ...), custom_call_target="tpu_custom_call" | custom-call | tf_op jit(solution)/shard_map/pallas_call | solution.py:912
Async XLA Ops:
  1.3 71.8 %copy-start.1 = (f32[1,2,192,768]{3,2,1,0:T(8,128)S(1)}, f32[1,2,192,768]{3,2,1,0:T(8,128)}, u32[]{:S(2)}) copy-start(f32[1,2,192,768]{3,2,1,0:T(8,128)} %param.21) | copy-start | bytes 3538948
  1.3 71.8 %copy-start.2 = (f32[1,2,768,192]{2,3,1,0:T(8,128)S(1)}, f32[1,2,768,192]{2,3,1,0:T(8,128)}, u32[]{:S(2)}) copy-start(f32[1,2,768,192]{2,3,1,0:T(8,128)} %param.23) | copy-start | bytes 3538948
  1.3 71.8 %copy-start.3 = (f32[1,2,192,49]{2,1,3,0:T(2,128)S(1)}, f32[1,2,192,49]{2,1,3,0:T(2,128)}, u32[]{:S(2)}) copy-start(f32[1,2,192,49]{2,1,3,0:T(2,128)} %param.18) | copy-start | bytes 225796
  73.1 1.3 %copy-start = (bf16[2,2,8,10,16,128]{5,4,3,2,1,0:T(8,128)(2,1)S(1)}, bf16[2,2,8,10,16,128]{5,4,3,2,1,0:T(8,128)(2,1)}, u32[]{:S(2)}) copy-start(bf16[2,2,8,10,16,128]{5,4,3,2,1,0:T(8,128)(2,1)} %shard_map.173.totals) | copy-start | bytes 3932164

commit v5 on v4

--- a/solution.py
+++ b/solution.py
@@ -28,6 +28,8 @@
 XY = 8
 EW = 8
 SHIFTED = (0, 1, 2, 4, 5, 6)
+PLANE_ORDER = [2, 6, 1, 3, 5, 7, 4]
+LINE_ORDER = [4, 3, 5, 2, 6, 1, 7]
 NS = 16
 ZT = 2
 GAIN, SHIFT, OUT_BIAS, SCALE = 49, 50, 51, 52
@@ -320,7 +322,7 @@
         core = self.place.core
         self.pack(grads, 1 - core, self.send1)
         self.first = []
-        for step in list(range(1, XY)) + [0]:
+        for step in PLANE_ORDER + [0]:
             part = self.share(step)
             copy = remote(
                 self.send1.at[part], self.recv1.at[part], *self.pair(0, step), self.place.twin()
@@ -357,7 +359,7 @@
 
     def extra_to_plane(self):
         self.extra.wait_recv()
-        for step in list(range(1, XY)) + [0]:
+        for step in PLANE_ORDER + [0]:
             spot = 72 + self.chunk(step)
             part = self.own[spot] + self.recv1[spot].astype(F32)
             if step == 0:
@@ -391,7 +393,9 @@
                 *self.pair(2, step - 1),
                 self.place.on_line(step),
             )
-            self.third.append(self.go(copy))
+            self.third.append(copy)
+        for step in LINE_ORDER:
+            self.go(self.third[step - 1])
 
     def back_line(self):
         for copy in self.third:
@@ -404,7 +408,9 @@
         self.fourth = []
         for step in range(1, EW):
             copy = remote(here, here, *self.pair(3, step - 1), self.place.on_line(step))
-            self.fourth.append(self.go(copy))
+            self.fourth.append(copy)
+        for step in LINE_ORDER:
+            self.go(self.fourth[step - 1])
 
     def back_plane(self):
         for copy in self.fourth:

time: 76.3 us -> 74.6 us (0.978)
  Pallas kernels: 73.5 us -> 71.8 us
    pallas_call x1, Pallas kernels: 71.8 us -> 70.1 us  [whole_step(): pl.pallas_call(step_kernel, out_shape=jax.ShapeDtypeStruct((LAYERS, 2, XY...]
where the time goes in v5:
time: 74.6 us; the launch traced here: 74.5 us
  Pallas kernels  71.8 us (96%)
  between operations  1.35 us (2%)
  local copies, waits for them, and re-layouts  1.32 us (2%)
    pallas_call x1, Pallas kernels, whole_step(): pl.pallas_call(step_kernel, out_shape=jax.ShapeDtypeStruct((LAYERS, 2, XY...  70.1 us
    pallas_call x1, Pallas kernels, update(): pl.pallas_call(update_kernel, out_shape=[weights, weights, jax.ShapeDtype...  1.71 us

profile of v5, /device:TPU:1, one launch (start us, length us, event | category | flops | bytes accessed | tf_op | source)
XLA Modules:
  0.0 74.5 jit_solution(11813127734420837816)
XLA Ops:
  1.3 0.0 copy-start.1
  1.3 0.0 copy-start.2
  1.3 0.0 copy-start.3
  1.3 70.1 %shard_map.173.totals = bf16[2,2,8,10,16,128]{5,4,3,2,1,0:T(8,128)(2,1)} custom-call(s32[1]{0:T(128)S(6)} %copy.19.index, bf16[768,128]{1,0:T(8,128)(2,1)} %bitcast.33, bf16[768,128]{1,0:T(8,128)(2,1)} %bitcast.34, s32[4,128]{1,0:T(4,128)} %mask_in.1, f32[49,2,192]{2,1,0:T(2,128)} %bitcast.30, f32[2,192]{1,0:T(2,128)} %bitcast.36, f32[2,192]{1,0:T(2,128)} %bitcast.37, ...), custom_call_target="tpu_custom_call" | custom-call | tf_op jit(solution)/shard_map/pallas_call | solution.py:824
  71.4 0.0 copy-done.1
  71.5 0.0 copy-done.2
  71.5 0.0 copy-done.3
  71.5 0.0 copy-start
  71.5 1.3 %copy-done = bf16[2,2,8,10,16,128]{5,4,3,2,1,0:T(8,128)(2,1)S(1)} copy-done((bf16[2,2,8,10,16,128]{5,4,3,2,1,0:T(8,128)(2,1)S(1)}, bf16[2,2,8,10,16,128]{5,4,3,2,1,0:T(8,128)(2,1)}, u32[]{:S(2)}) %copy-start) | copy-done | bytes 1310744
  72.8 1.7 %shard_map.174 = (f32[2,192,768]{2,1,0:T(8,128)}, f32[2,192,768]{2,1,0:T(8,128)}, f32[49,2,192]{2,1,0:T(2,128)}, f32[64,192]{1,0:T(8,128)}, f32[64,192]{1,0:T(8,128)}) custom-call(bf16[2,2,8,10,16,128]{5,4,3,2,1,0:T(8,128)(2,1)S(1)} %copy-done, f32[2,192,768]{2,1,0:T(8,128)S(1)} %bitcast.27, f32[2,192,768]{2,1,0:T(8,128)S(1)} %bitcast.29, ...), custom_call_target="tpu_custom_call" | custom-call | tf_op jit(solution)/shard_map/pallas_call | solution.py:918
Async XLA Ops:
  1.3 70.2 %copy-start.1 = (f32[1,2,192,768]{3,2,1,0:T(8,128)S(1)}, f32[1,2,192,768]{3,2,1,0:T(8,128)}, u32[]{:S(2)}) copy-start(f32[1,2,192,768]{3,2,1,0:T(8,128)} %param.21) | copy-start | bytes 3538948
  1.3 70.2 %copy-start.2 = (f32[1,2,768,192]{2,3,1,0:T(8,128)S(1)}, f32[1,2,768,192]{2,3,1,0:T(8,128)}, u32[]{:S(2)}) copy-start(f32[1,2,768,192]{2,3,1,0:T(8,128)} %param.23) | copy-start | bytes 3538948
  1.3 70.2 %copy-start.3 = (f32[1,2,192,49]{2,1,3,0:T(2,128)S(1)}, f32[1,2,192,49]{2,1,3,0:T(2,128)}, u32[]{:S(2)}) copy-start(f32[1,2,192,49]{2,1,3,0:T(2,128)} %param.18) | copy-start | bytes 225796
  71.5 1.3 %copy-start = (bf16[2,2,8,10,16,128]{5,4,3,2,1,0:T(8,128)(2,1)S(1)}, bf16[2,2,8,10,16,128]{5,4,3,2,1,0:T(8,128)(2,1)}, u32[]{:S(2)}) copy-start(bf16[2,2,8,10,16,128]{5,4,3,2,1,0:T(8,128)(2,1)} %shard_map.173.totals) | copy-start | bytes 3932164
